TPU v7x, 128 devices: a whole 4x4x4 slice. The times are simulated.
128 devices in a mesh: rep: 4 (over x_lo, core), fsdp: 32 (over z, y, x_hi).
Axes of the slice: x: 4 (x_hi: 2, x_lo: 2; x = x_hi * 2 + x_lo), y: 4, z: 4, core: 2. Of those that a mesh axis runs over, the one named last changes fastest.
Arguments:
- tokens: bfloat16 [4, 32768, 5120], P('rep', 'fsdp'), may hold values from -6 to 6
- targets: int32 [4, 32768], P('rep', 'fsdp'), may hold values from 0 to 1023
- norm_gain: float32 [5120], replicated, may hold values from 0.5 to 1.5
- weights: float32 [4, 5120, 1024], P('rep', 'fsdp'), may hold values from -6 to 6
- anchor: float32 [5120, 1024], P('fsdp', 'rep'), may hold values from -6 to 6
- momentum: float32 [5120, 1024], P('fsdp', 'rep'), may hold values from -2 to 2
- step_index: int32 [1], replicated, may hold values from 0 to 99999
- frag_table: int32 [8], replicated, may hold values from 0 to 7, each once
Outputs:
- token_loss: float32 [4, 32768], P('rep', 'fsdp')
- weights_out: float32 [4, 5120, 1024], P('rep', 'fsdp')
- momentum_out: float32 [5120, 1024], P('fsdp', 'rep')
All inputs are finite; a program needn't handle non-finite values.
Results may differ from a plain program's by a relative error of at most 0.0025.
Values may be sent and summed in bfloat16 or wider, within the bound.
A program may use at most 128 MiB of HBM per device.

v0:
```python
import jax
import jax.numpy as jnp
from jax import lax
from jax.sharding import PartitionSpec as P


def on_device(tokens, targets, norm_gain, weights, anchor, momentum, step_index, frag_table):
    xf = tokens[0].astype(jnp.float32)
    ms = jnp.mean(xf * xf, axis=-1, keepdims=True)
    normed = (xf * lax.rsqrt(ms + 1e-05) * norm_gain).astype(jnp.bfloat16)
    vocab = weights.shape[2]
    width = tokens.shape[2]
    scale = 1.0 / jnp.sqrt(jnp.float32(width))
    head = weights[0].astype(jnp.bfloat16)
    columns = normed
    logits = (
        jnp.dot(
            columns,
            lax.all_gather(head, "fsdp", axis=0, tiled=True),
            preferred_element_type=jnp.float32,
        )
        * scale
    )
    expo = jnp.exp(logits)
    total = jnp.sum(expo, axis=-1)
    onehot = jnp.arange(vocab, dtype=jnp.int32)[None, :] == targets[0][:, None]
    picked = jnp.sum(jnp.where(onehot, logits, 0.0), axis=-1)
    loss = jnp.log(total) - picked
    err = (expo / total[:, None] - onehot.astype(jnp.float32)).astype(jnp.bfloat16)
    local_rows = weights.shape[1]
    columns = normed
    grad = lax.psum_scatter(
        (jnp.dot(columns.T, err, preferred_element_type=jnp.float32) * scale).astype(jnp.bfloat16),
        "fsdp",
        scatter_dimension=0,
        tiled=True,
    ).astype(jnp.float32)
    stepped = weights[0] - 1.0 * grad
    frag_count = frag_table.shape[0]
    pos = step_index[0] % frag_count
    frag = jnp.sum(jnp.where(jnp.arange(frag_count, dtype=jnp.int32) == pos, frag_table, 0))
    run_rows = local_rows // frag_count
    offset = frag * run_rows
    replicas = lax.axis_size("rep")
    own_rows = lax.dynamic_slice_in_dim(stepped, offset, run_rows, 0)
    anchor_rows = lax.dynamic_slice_in_dim(anchor, offset, run_rows, 0)
    moment_rows = lax.dynamic_slice_in_dim(momentum, offset, run_rows, 0)
    summed = lax.psum_scatter(own_rows, "rep", scatter_dimension=1, tiled=True)
    delta = anchor_rows - summed / replicas
    mom_slice = 0.9 * moment_rows + delta
    part_rows = anchor_rows - 0.7 * (delta + 0.9 * mom_slice)
    new_rows = lax.all_gather(part_rows, "rep", axis=1, tiled=True)
    weights_out = lax.dynamic_update_slice_in_dim(stepped, new_rows, offset, 0)
    momentum_out = lax.dynamic_update_slice_in_dim(momentum, mom_slice, offset, 0)
    return (loss[None], weights_out[None], momentum_out)


def solution(mesh):
    return jax.shard_map(
        on_device,
        mesh=mesh,
        in_specs=(
            P("rep", "fsdp", None),
            P("rep", "fsdp"),
            P(),
            P("rep", "fsdp", None),
            P("fsdp", "rep"),
            P("fsdp", "rep"),
            P(),
            P(),
        ),
        out_specs=(P("rep", "fsdp"), P("rep", "fsdp", None), P("fsdp", "rep")),
        check_vma=False,
    )
```

profile of v0, /device:TPU:1, one launch (start us, length us, event | category | flops | bytes accessed | tf_op | source)
XLA Modules:
  0.0 433.6 jit_solution(10200668860572339493)
XLA Ops:
  7.2 0.0 copy-start.4
  7.2 0.0 copy-start.3
  7.2 0.0 all-gather.2.cloned.1.call-start
  7.2 0.9 copy.15
  8.1 1.9 bitcast_convert_fusion
  10.0 0.0 all-gather.2.cloned.1.call-update
  10.0 0.0 reduce-scatter.3.cloned.1.call-start
  10.1 6.1 %fusion = f32[1024]{0:T(1024)S(1)} fusion(bf16[1,1024,5120]{2,1,0:T(8,128)(2,1)} %param.8), kind=kLoop, calls=%fused_computation.2 | loop fusion | flops 15727616 | bytes 10489856 | tf_op jit(solution)/shard_map/reduce_sum | solution.py:9
  16.2 115.5 %all-gather.2.cloned.1.call-done = bf16[5120,1024]{1,0:T(8,128)(2,1)} async-done(((bf16[160,1024]{1,0:T(8,128)(2,1)}), bf16[5120,1024]{1,0:T(8,128)(2,1)}) %all-gather.2.cloned.1.call-update) | async-done | bytes 10485776 | tf_op jit(solution)/shard_map/all_gather | solution.py:19
  131.7 0.0 copy-done.4
  131.7 0.0 copy-done.3
  131.7 19.0 %exponential_reduce_fusion = (f32[1024]{0:T(1024)S(1)}, f32[1024]{0:T(1024)S(1)}, f32[1024,1024]{0,1:T(8,128)}) fusion(s32[1024]{0:T(1024)S(1)} %bitcast.23, bf16[5120,1024]{1,0:T(8,128)(2,1)} %all-gather.2.cloned.1.call-done, bf16[1,1024,5120]{2,1,0:T(8,128)(2,1)} %param.8, f32[5120]{0:T(1024)S(1)} %copy-done.3, f32[1024]{0:T(1024)S(1)} %add_rsqrt_fusion), kind=kOutput, calls=%fused_computation.9 | convolution fusion | flops 10763630592 | bytes 25202688 | tf_op jit(solution)/shard_map/dot_general | solution.py:17
  150.7 18.7 %multiply_convert_fusion = bf16[5120,1024]{1,0:T(8,128)(2,1)} fusion(bf16[1,1024,5120]{2,1,0:T(8,128)(2,1)} %param.8, f32[5120]{0:T(1024)S(1)} %copy-done.3, f32[1024]{0:T(1024)S(1)} %add_rsqrt_fusion, f32[1024,1024]{0,1:T(8,128)} %get-tuple-element.7, f32[1024]{0:T(1024)S(1)} %get-tuple-element.3, s32[1024]{0:T(1024)S(1)} %bitcast.24), kind=kOutput, calls=%fused_computation.5 | convolution fusion | flops 10775166976 | bytes 25198592 | tf_op jit(solution)/shard_map/dot_general | solution.py:33
  169.4 0.0 reduce-scatter.3.cloned.1.call-update
  169.4 0.0 reduce-scatter.5.cloned.1.call-start
  170.2 0.0 copy-done.5
  170.2 0.6 fusion.9
  171.5 230.9 %reduce-scatter.3.cloned.1.call-done = bf16[160,1024]{1,0:T(8,128)(2,1)} async-done(((bf16[5120,1024]{1,0:T(8,128)(2,1)}), bf16[160,1024]{1,0:T(8,128)(2,1)}) %reduce-scatter.3.cloned.1.call-update) | async-done | bytes 327696 | tf_op jit(solution)/shard_map/reduce_scatter | solution.py:32
  402.4 0.0 copy-done
  402.4 1.1 bitcast_subtract_fusion
  403.4 0.7 constant_dynamic-slice_fusion
  404.1 0.0 reduce-scatter.5.cloned.1.call-update
  404.1 0.6 log_subtract_fusion
  404.7 14.6 %reduce-scatter.5.cloned.1.call-done = f32[20,256]{1,0:T(8,128)} async-done(((f32[20,1024]{1,0:T(8,128)}), f32[20,256]{1,0:T(8,128)}) %reduce-scatter.5.cloned.1.call-update) | async-done | bytes 20496 | tf_op jit(solution)/shard_map/reduce_scatter | solution.py:48
  419.4 0.8 multiply_subtract_fusion
  420.1 5.3 %all_gather.7 = f32[20,1024]{1,0:T(8,128)S(1)} all-gather(f32[20,256]{1,0:T(8,128)S(1)} %get-tuple-element.5), channel_id=1, replica_groups=mesh['rep'=4,'fsdp'=32] {'rep'}, dimensions={1}, use_global_device_ids=true | all-gather | bytes 102400 | tf_op jit(solution)/shard_map/all_gather | solution.py:52
  425.5 0.2 dynamic_update_slice.8
  425.7 0.0 copy-start.2
  425.7 0.5 dynamic_update_slice.7
  426.2 0.0 copy-start.1
  426.2 0.1 copy-done.2
  426.3 0.7 copy-done.1
  (3 shorter events, 0.0 us)
Async XLA Ops:
  7.2 124.5 %copy-start.4 = (s32[1,1024]{1,0:T(1,128)S(1)}, s32[1,1024]{1,0:T(1,128)}, u32[]{:S(2)}) copy-start(s32[1,1024]{1,0:T(1,128)} %param.9) | copy-start | bytes 12292
  7.2 124.5 %copy-start.3 = (f32[5120]{0:T(1024)S(1)}, f32[5120]{0:T(1024)}, u32[]{:S(2)}) copy-start(f32[5120]{0:T(1024)} %param.10) | copy-start | bytes 61444
  7.2 124.5 %all-gather.2.cloned.1.call-start = ((), (), s32[]{:S(2)}) async-start(), calls=%async_computation.2 | async-start | bytes 10813440 | tf_op jit(solution)/shard_map/all_gather | solution.py:19
  10.0 392.3 %reduce-scatter.3.cloned.1.call-start = ((), (), s32[]{:S(2)}) async-start(), calls=%async_computation.3 | async-start | bytes 10813440 | tf_op jit(solution)/shard_map/reduce_scatter | solution.py:32
  169.4 0.8 copy-start.5
  169.4 232.9 %copy-start = (f32[1,160,1024]{2,1,0:T(8,128)S(1)}, f32[1,160,1024]{2,1,0:T(8,128)}, u32[]{:S(2)}) copy-start(f32[1,160,1024]{2,1,0:T(8,128)} %param.11) | copy-start | bytes 1966084
  169.4 249.9 %reduce-scatter.5.cloned.1.call-start = ((), (), s32[]{:S(2)}) async-start(), calls=%async_computation.4 | async-start | bytes 122880 | tf_op jit(solution)/shard_map/reduce_scatter | solution.py:48
  425.7 0.7 copy-start.2
  426.2 0.8 copy-start.1
Sparse Core Ops, SparseCore 0:
  11.7 119.8 all-gather.1
  169.6 232.7 reduce-scatter.2
  405.3 14.0 reduce-scatter.4
where the time goes:
time: 434 us
  waiting for transfers between devices  361 us (83%)
  matrix products  37.7 us (9%)
  between operations  15.2 us (4%)
  other arithmetic  11 us (3%)
  blocking collectives  5.32 us (1%)
    reduce_scatter x1, waiting for transfers between devices, on_device(): lax.psum_scatter((jnp.dot(columns.T, err, preferred_element_type=jnp.floa...  231 us
    all_gather x1, waiting for transfers between devices, on_device(): lax.all_gather(head, 'fsdp', axis=0, tiled=True)  115 us
    dot_general x1, matrix products, on_device(): jnp.dot(columns, lax.all_gather(head, 'fsdp', axis=0, tiled=True), prefer...  19 us
    dot_general x1, matrix products, on_device(): jnp.dot(columns.T, err, preferred_element_type=jnp.float32) * scale  18.7 us
    reduce_scatter x1, waiting for transfers between devices, on_device(): summed = lax.psum_scatter(own_rows, 'rep', scatter_dimension=1, tiled=True)  14.6 us
  transfers between devices with their start and end apart: 3, of which 3 were waited for; matrix products, arithmetic and copies ran while one was open for 2% of the time, Pallas kernels for 0%

commit v1 on v0

v1 whole, which is shorter than its diff:
```python
import functools

import jax
import jax.numpy as jnp
import numpy as np
from jax import lax
from jax.experimental import pallas as pl
from jax.experimental.pallas import tpu as pltpu
from jax.sharding import PartitionSpec as P

F32 = jnp.float32
BF16 = jnp.bfloat16
MESH = pl.DeviceIdType.MESH

GATHER_ORDER = (0, 2, 6, 1, 4, 3, 7, 5)
SCATTER_ORDER = (5, 7, 3, 4, 1, 6, 2, 0)


def dot(a, b, ca, cb):
    return lax.dot_general(a, b, (((ca,), (cb,)), ((), ())), preferred_element_type=F32)


def kernel(
    tokens, targets, gain, weights, anchor, momentum, step_index, frag_table,
    loss_out, weights_out, momentum_out,
    head, normed_t, grad, logits_t, err_t, tok, rq_half, rq, rx, rp_half, rp, stepped, rows_out, rows_in, new_out, new_in,
    tok_sem, gp_s, gp_r, gx_s, gx_r, gq_s, gq_r, sp_s, sp_r, sx_s, sx_r, sq_s, sq_r, e_s, e_r, n_s, n_r,
):
    rows, vocab = weights.shape
    half = rows // 2
    count, width = tokens.shape[1:]
    frag_count = frag_table.shape[0]
    run = rows // frag_count
    chunk = tok.shape[1]
    scale = np.float32(1.0 / np.sqrt(np.float32(width)))

    r, f = lax.axis_index("rep"), lax.axis_index("fsdp")
    core = r % 2
    z, y, x = f // 8, (f // 2) % 4, f % 2
    p = jnp.where(core == 0, z, y)
    q = jnp.where(core == 0, y, z)

    def device(dp=0, dq=0, dx=0):
        pp, qq, xx = (p + dp) % 4, (q + dq) % 4, (x + dx) % 2
        return (r, jnp.where(core == 0, pp, qq) * 8 + jnp.where(core == 0, qq, pp) * 2 + xx)

    p_up, p_down, q_up, q_down, x_other = device(dp=1), device(dp=3), device(dq=1), device(dq=3), device(dx=1)

    def sibling(j):
        c2, l2 = (core + j) % 2, (r // 2 + j // 2) % 2
        return l2 * 2 + c2

    siblings = [(sibling(j), f) for j in (1, 2, 3)]

    barrier = pltpu.get_barrier_semaphore()
    partners = [p_up, p_down, q_up, q_down, x_other] + siblings
    for partner in partners:
        pl.semaphore_signal(barrier, inc=1, device_id=partner, device_id_type=MESH)

    chunks = count // chunk
    slots = tok.shape[0]

    def token_copy(c):
        return pltpu.make_async_copy(
            tokens.at[0, pl.ds(c * chunk, chunk)], tok.at[c % slots], tok_sem.at[c % slots]
        )

    for c in range(slots):
        token_copy(c).start()
    head[0, pl.ds(0, rows)] = weights[...].astype(BF16)
    pl.semaphore_wait(barrier, len(partners))

    sent = []

    def send(src, dst, s_sem, r_sem, to):
        copy = pltpu.make_async_remote_copy(
            src_ref=src, dst_ref=dst, send_sem=s_sem, recv_sem=r_sem, device_id=to, device_id_type=MESH
        )
        copy.start()
        sent.append(copy)
        return copy

    whole = lambda dq: pl.ds(dq * rows, rows)
    low = lambda dq: pl.ds(dq * rows, half)
    high = lambda dq: pl.ds(dq * rows + half, half)

    def gather_q(i):
        a = send(head.at[i, whole(0)], head.at[i, whole(3)], gq_s.at[i, 0], gq_r.at[i, 0], q_up)
        b = send(head.at[i, whole(0)], head.at[i, whole(1)], gq_s.at[i, 1], gq_r.at[i, 1], q_down)
        return a, b

    def forward_q(i, pair):
        pair[0].wait_recv()
        a = send(head.at[i, low(3)], head.at[i, low(2)], gq_s.at[i, 2], gq_r.at[i, 2], q_up)
        pair[1].wait_recv()
        b = send(head.at[i, high(1)], head.at[i, high(2)], gq_s.at[i, 3], gq_r.at[i, 3], q_down)
        return a, b

    def gather_x(dp):
        return send(head.at[2 * dp, whole(0)], head.at[2 * dp + 1, whole(0)], gx_s.at[dp], gx_r.at[dp], x_other)

    def norm_chunk(c, slot):
        xf = tok[slot].astype(F32)
        inv = lax.rsqrt(jnp.sum(xf * xf, axis=1, keepdims=True) * np.float32(1.0 / width) + np.float32(1e-5))

        def unit(j, carry):
            columns = pl.ds(pl.multiple_of(j * 4 * rows, 128), 4 * rows)
            part = (tok[slot, :, columns].astype(F32) * inv * gain[:, columns]).astype(BF16).T
            for b in range(4):
                bz, by, bx = j // 2, 2 * (j % 2) + b // 2, b % 2
                dp = (jnp.where(core == 0, bz, by) - p + 4) % 4
                dq = (jnp.where(core == 0, by, bz) - q + 4) % 4
                dx = (bx + x) % 2
                normed_t[
                    2 * dp + dx,
                    pl.ds(pl.multiple_of(dq * rows, 16), rows),
                    pl.ds(pl.multiple_of(c * chunk, chunk), chunk),
                ] = part[b * rows : (b + 1) * rows]
            return carry

        lax.fori_loop(0, width // (4 * rows), unit, 0)

    def norm(first, last):
        for c in range(first, last):
            token_copy(c).wait()
            norm_chunk(c, c % slots)
            if c + slots < chunks:
                token_copy(c + slots).start()

    tile = 256

    def add_logits(i, fresh):
        def step(j, carry):
            s = pl.ds(pl.multiple_of(j * tile, tile), tile)
            term = dot(head[i, :, s], normed_t[i], 0, 0)
            if fresh:
                logits_t[s, :] = term
            else:
                logits_t[s, :] += term
            return carry

        lax.fori_loop(0, vocab // tile, step, 0)

    own = head.at[0, whole(0)]
    up = send(own, head.at[6, whole(0)], gp_s.at[0], gp_r.at[0], p_up)
    down = send(own, head.at[2, whole(0)], gp_s.at[1], gp_r.at[1], p_down)
    gx = {0: gather_x(0)}
    gq, fq = {0: gather_q(0)}, {}
    norm(0, 4)
    up.wait_recv()
    up2 = send(head.at[6, low(0)], head.at[4, low(0)], gp_s.at[2], gp_r.at[2], p_up)
    down.wait_recv()
    down2 = send(head.at[2, high(0)], head.at[4, high(0)], gp_s.at[3], gp_r.at[3], p_down)
    gx[1] = gather_x(1)
    gx[3] = gather_x(3)
    gq[2] = gather_q(2)
    gq[6] = gather_q(6)
    gx[0].wait_recv()
    gq[1] = gather_q(1)
    norm(4, 6)
    fq[0] = forward_q(0, gq[0])
    up2.wait_recv()
    down2.wait_recv()
    gx[2] = gather_x(2)
    gq[4] = gather_q(4)
    norm(6, 8)
    fq[2] = forward_q(2, gq[2])
    fq[6] = forward_q(6, gq[6])

    def finish(i, fresh=False):
        fq[i][0].wait_recv()
        fq[i][1].wait_recv()
        add_logits(i, fresh)

    finish(0, True)
    gx[1].wait_recv()
    gq[3] = gather_q(3)
    gx[3].wait_recv()
    gq[7] = gather_q(7)
    fq[1] = forward_q(1, gq[1])
    finish(2)
    gx[2].wait_recv()
    gq[5] = gather_q(5)
    fq[4] = forward_q(4, gq[4])
    finish(6)
    fq[3] = forward_q(3, gq[3])
    finish(1)
    fq[7] = forward_q(7, gq[7])
    finish(4)
    fq[5] = forward_q(5, gq[5])
    finish(3)
    finish(7)
    finish(5)

    lanes = 128

    def soften(j, carry):
        s = pl.ds(pl.multiple_of(j * lanes, lanes), lanes)
        logit = logits_t[:, s] * scale
        expo = jnp.exp(logit)
        total = jnp.sum(expo, axis=0, keepdims=True)
        onehot = lax.broadcasted_iota(jnp.int32, (vocab, lanes), 0) == targets[:, s]
        picked = jnp.sum(jnp.where(onehot, logit, 0.0), axis=0, keepdims=True)
        loss_out[:, s] = jnp.log(total) - picked
        err_t[:, s] = (expo * (1.0 / total) - jnp.where(onehot, 1.0, 0.0)).astype(BF16)
        return carry

    lax.fori_loop(0, count // lanes, soften, 0)

    def term(i, dq):
        grad[i, whole(dq)] = (dot(normed_t[i, whole(dq)], err_t[...], 1, 1) * scale).astype(BF16)

    def start_terms(i):
        term(i, 2)
        a = send(grad.at[i, low(2)], rq_half.at[i, 0], sq_s.at[i, 0], sq_r.at[i, 0], q_up)
        b = send(grad.at[i, high(2)], rq_half.at[i, 1], sq_s.at[i, 1], sq_r.at[i, 1], q_down)
        term(i, 1)
        term(i, 3)
        term(i, 0)
        return a, b

    def add_into(i, where, *others):
        total = grad[i, where].astype(F32)
        for other in others:
            total = total + other[...].astype(F32)
        grad[i, where] = total.astype(BF16)

    def pass_on(i, pair):
        pair[0].wait_recv()
        add_into(i, low(1), rq_half.at[i, 0])
        a = send(grad.at[i, whole(1)], rq.at[i, 0], sq_s.at[i, 2], sq_r.at[i, 2], q_up)
        pair[1].wait_recv()
        add_into(i, high(3), rq_half.at[i, 1])
        b = send(grad.at[i, whole(3)], rq.at[i, 1], sq_s.at[i, 3], sq_r.at[i, 3], q_down)
        return a, b

    halves, wholes, sx = {}, {}, {}
    p_half, p_whole = [], {}

    def settle(i):
        for copy in wholes[i]:
            copy.wait_recv()
        dp, dx = i // 2, i % 2
        if dx:
            add_into(i, whole(0), rq.at[i, 0], rq.at[i, 1])
            sx[dp] = send(grad.at[i, whole(0)], rx.at[dp], sx_s.at[dp], sx_r.at[dp], x_other)
        elif dp == 2:
            sx[2].wait_recv()
            add_into(i, whole(0), rq.at[i, 0], rq.at[i, 1], rx.at[2])
            p_half.append(send(grad.at[i, low(0)], rp_half.at[0], sp_s.at[0], sp_r.at[0], p_up))
            p_half.append(send(grad.at[i, high(0)], rp_half.at[1], sp_s.at[1], sp_r.at[1], p_down))
        elif dp:
            sx[dp].wait_recv()
            add_into(i, whole(0), rq.at[i, 0], rq.at[i, 1], rx.at[dp])
            if dp == 1:
                p_half[0].wait_recv()
                add_into(i, low(0), rp_half.at[0])
                p_whole[0] = send(grad.at[i, whole(0)], rp.at[0], sp_s.at[2], sp_r.at[2], p_up)
            else:
                p_half[1].wait_recv()
                add_into(i, high(0), rp_half.at[1])
                p_whole[1] = send(grad.at[i, whole(0)], rp.at[1], sp_s.at[3], sp_r.at[3], p_down)

    order = SCATTER_ORDER
    halves[order[0]] = start_terms(order[0])
    for k, i in enumerate(order):
        if k + 1 < len(order):
            halves[order[k + 1]] = start_terms(order[k + 1])
        wholes[i] = pass_on(i, halves[i])
        if k:
            settle(order[k - 1])
    for copy in wholes[0]:
        copy.wait_recv()
    sx[0].wait_recv()
    total = grad[0, whole(0)].astype(F32)
    for part in (rq.at[0, 0], rq.at[0, 1], rx.at[0]):
        total = total + part[...].astype(F32)
    for k in (1, 0):
        p_whole[k].wait_recv()
        total = total + rp[k].astype(F32)
    stepped[pl.ds(0, rows)] = weights[...] - total
    stepped[pl.ds(rows, 8)] = jnp.zeros((8, vocab), F32)

    pos = step_index[0] % frag_count
    frag = jnp.int32(0)
    for k in range(frag_count):
        frag = frag + jnp.where(pos == k, frag_table[k], 0)
    pad = rows_out.shape[1]
    part = vocab // 4
    mine = jnp.zeros((pad, vocab), F32)
    for k in range(frag_count):
        mine = jnp.where(frag == k, stepped[pl.ds(k * run, pad)], mine)
    for k in range(4):
        rows_out[k] = mine[:, k * part : (k + 1) * part]
    exchange = [
        send(rows_out.at[to[0]], rows_in.at[j], e_s.at[j], e_r.at[j], to) for j, to in enumerate(siblings)
    ]
    held = jnp.zeros((run, part), F32)
    moment = jnp.zeros((run, part), F32)
    for k in range(frag_count):
        held = jnp.where(frag == k, anchor[pl.ds(k * run, run)], held)
        moment = jnp.where(frag == k, momentum[pl.ds(k * run, run)], moment)
    summed = rows_out[r]
    for j, copy in enumerate(exchange):
        copy.wait_recv()
        summed = summed + rows_in[j]
    delta = held - summed[:run] / 4
    moment = 0.9 * moment + delta
    fresh_rows = held - 0.7 * (delta + 0.9 * moment)
    new_out[pl.ds(0, run)] = fresh_rows
    new_out[pl.ds(run, pad - run)] = jnp.zeros((pad - run, part), F32)
    spread = [send(new_out, new_in.at[j], n_s.at[j], n_r.at[j], to) for j, to in enumerate(siblings)]
    for k in range(frag_count):
        s = pl.ds(k * run, run)
        momentum_out[s] = jnp.where(frag == k, moment, momentum[s])
        weights_out[s, pl.ds(pl.multiple_of(r * part, part), part)] = jnp.where(
            frag == k, fresh_rows, stepped[s, pl.ds(pl.multiple_of(r * part, part), part)]
        )
    for j, copy in enumerate(spread):
        copy.wait_recv()
        columns = pl.ds(pl.multiple_of(siblings[j][0] * part, part), part)
        for k in range(frag_count):
            s = pl.ds(k * run, run)
            weights_out[s, columns] = jnp.where(frag == k, new_in[j, pl.ds(0, run)], stepped[s, columns])
    for copy in sent:
        copy.wait_send()


def on_device(tokens, targets, norm_gain, weights, anchor, momentum, step_index, frag_table):
    _, count, width = tokens.shape
    _, rows, vocab = weights.shape
    half = rows // 2
    part = vocab // 4
    run = rows // frag_table.shape[0]
    pad = -(-run // 8) * 8
    vmem = pl.BlockSpec(memory_space=pltpu.VMEM)
    smem = pl.BlockSpec(memory_space=pltpu.SMEM)
    dma = pltpu.SemaphoreType.DMA
    big = pltpu.VMEM((8, 4 * rows, vocab), BF16)
    loss, weights_out, momentum_out = pl.pallas_call(
        kernel,
        out_shape=(
            jax.ShapeDtypeStruct((1, count), F32),
            jax.ShapeDtypeStruct((rows, vocab), F32),
            jax.ShapeDtypeStruct((rows, part), F32),
        ),
        in_specs=[pl.BlockSpec(memory_space=pl.ANY)] + [vmem] * 5 + [smem] * 2,
        out_specs=(vmem, vmem, vmem),
        scratch_shapes=[
            big,
            pltpu.VMEM((8, 4 * rows, count), BF16),
            big,
            pltpu.VMEM((vocab, count), F32),
            pltpu.VMEM((vocab, count), BF16),
            pltpu.VMEM((4, 128, width), BF16),
            pltpu.VMEM((8, 2, half, vocab), BF16),
            pltpu.VMEM((8, 2, rows, vocab), BF16),
            pltpu.VMEM((4, rows, vocab), BF16),
            pltpu.VMEM((2, half, vocab), BF16),
            pltpu.VMEM((2, rows, vocab), BF16),
            pltpu.VMEM((rows + 8, vocab), F32),
            pltpu.VMEM((4, pad, part), F32),
            pltpu.VMEM((3, pad, part), F32),
            pltpu.VMEM((pad, part), F32),
            pltpu.VMEM((3, pad, part), F32),
            dma((4,)),
            dma((4,)), dma((4,)), dma((4,)), dma((4,)), dma((8, 4)), dma((8, 4)),
            dma((4,)), dma((4,)), dma((4,)), dma((4,)), dma((8, 4)), dma((8, 4)),
            dma((3,)), dma((3,)), dma((3,)), dma((3,)),
        ],
        compiler_params=pltpu.CompilerParams(
            collective_id=0, has_side_effects=True, vmem_limit_bytes=62 * 1024 * 1024
        ),
    )(
        tokens, targets, norm_gain[None], weights[0], anchor, momentum, step_index, frag_table
    )
    return (loss, weights_out[None], momentum_out)


def solution(mesh):
    return jax.shard_map(
        on_device,
        mesh=mesh,
        in_specs=(
            P("rep", "fsdp", None),
            P("rep", "fsdp"),
            P(),
            P("rep", "fsdp", None),
            P("fsdp", "rep"),
            P("fsdp", "rep"),
            P(),
            P(),
        ),
        out_specs=(P("rep", "fsdp"), P("rep", "fsdp", None), P("fsdp", "rep")),
        check_vma=False,
    )
```

time: 434 us -> 136 us (0.31)
  waiting for transfers between devices: 361 us -> 0 us
  Pallas kernels: 0 us -> 130 us
  matrix products: 37.7 us -> 0 us
  between operations: 15.2 us -> 1.29 us
  other arithmetic: 11 us -> 0 us
  blocking collectives: 5.32 us -> 0 us
    reduce_scatter x2 -> x0, waiting for transfers between devices: 245 us -> none  [the longest x1 231 us: on_device(): lax.psum_scatter((jnp.dot(columns.T, err, preferred_element_type=jnp.floa...]
    pallas_call x0 -> x1, Pallas kernels: none -> 130 us  [on_device(): pl.pallas_call(kernel, out_shape=(jax.ShapeDtypeStruct((1, count), F32),...]
    all_gather x1 -> x0, waiting for transfers between devices: 115 us -> none  [on_device(): lax.all_gather(head, 'fsdp', axis=0, tiled=True)]
    dot_general x2 -> x0, matrix products: 37.7 us -> none  [the longest x1 19 us: on_device(): jnp.dot(columns, lax.all_gather(head, 'fsdp', axis=0, tiled=True), prefer...]
    reduce_sum x2 -> x0, other arithmetic: 6.73 us -> none  [the longest x1 6.1 us: on_device(): ms = jnp.mean(xf * xf, axis=-1, keepdims=True)]
    all_gather x1 -> x0, blocking collectives: 5.32 us -> none  [on_device(): new_rows = lax.all_gather(part_rows, 'rep', axis=1, tiled=True)]
  transfers between devices with their start and end apart: 3 -> 0, of which waited for: 3 -> 0; matrix products, arithmetic and copies ran while one was open for 2% -> 0% of each run, Pallas kernels for 0% -> 0%
where the time goes in v1:
time: 136 us
  Pallas kernels  130 us (96%)
  local copies, waits for them, and re-layouts  4.84 us (4%)
    pallas_call x1, Pallas kernels, on_device(): pl.pallas_call(kernel, out_shape=(jax.ShapeDtypeStruct((1, count), F32),...  130 us
    unnamed x3, local copies, waits for them, and re-layouts  4.84 us

profile of v1, /device:TPU:1, one launch (start us, length us, event | category | flops | bytes accessed | tf_op | source)
XLA Modules:
  0.0 136.2 jit_solution(7196345134095258676)
XLA Ops:
  1.3 130.1 %shard_map.103 = (f32[1,1024]{1,0:T(1,128)}, f32[160,1024]{1,0:T(8,128)}, f32[160,256]{1,0:T(8,128)}) custom-call(bf16[1,1024,5120]{2,1,0:T(8,128)(2,1)} %tokens.1, s32[1,1024]{1,0:T(1,128)} %targets.1, f32[1,5120]{1,0:T(1,128)} %bitcast.5, f32[160,1024]{1,0:T(8,128)} %bitcast.3, f32[160,256]{1,0:T(8,128)} %anchor.1, f32[160,256]{1,0:T(8,128)} %momentum.1, ...), custom_call_target="tpu_custom_call" | custom-call | tf_op jit(solution)/shard_map/pallas_call | solution.py:340
  131.4 1.3 copy.15
  132.6 2.0 %copy.16 = f32[1,160,1024]{2,1,0:T(8,128)} copy(f32[1,160,1024]{2,1,0:T(8,128)} %bitcast.4) | data formatting | bytes 1310720
  134.6 1.6 %copy.17 = f32[160,256]{1,0:T(8,128)} copy(f32[160,256]{1,0:T(8,128)} %get-tuple-element.14) | data formatting | bytes 327680

commit v2 on v1

--- a/solution.py
+++ b/solution.py
@@ -12,8 +12,8 @@
 BF16 = jnp.bfloat16
 MESH = pl.DeviceIdType.MESH
 
-GATHER_ORDER = (0, 2, 6, 1, 4, 3, 7, 5)
-SCATTER_ORDER = (5, 7, 3, 4, 1, 6, 2, 0)
+SCATTER_ORDER = (5, 7, 3, 1, 4, 6, 2, 0)
+NEAR = 64
 
 
 def dot(a, b, ca, cb):
@@ -22,9 +22,10 @@
 
 def kernel(
     tokens, targets, gain, weights, anchor, momentum, step_index, frag_table,
-    loss_out, weights_out, momentum_out,
-    head, normed_t, grad, logits_t, err_t, tok, rq_half, rq, rx, rp_half, rp, stepped, rows_out, rows_in, new_out, new_in,
-    tok_sem, gp_s, gp_r, gx_s, gx_r, gq_s, gq_r, sp_s, sp_r, sx_s, sx_r, sq_s, sq_r, e_s, e_r, n_s, n_r,
+    loss_out, stepped_out, fresh_out, moment_out,
+    head, normed_t, grad, logits_t, err_t, tok, rq_half, rq, rx, rx_far, rp_half, rp, stepped, rows_out, rows_in, new_out, new_in,
+    tok_sem, gp_s, gp_r, gx_s, gx_r, gf_s, gf_r, gq_s, gq_r,
+    sp_s, sp_r, sx_s, sx_r, sf_s, sf_r, sq_s, sq_r, e_s, e_r, n_s, n_r,
 ):
     rows, vocab = weights.shape
     half = rows // 2
@@ -80,24 +81,39 @@
         sent.append(copy)
         return copy
 
-    whole = lambda dq: pl.ds(dq * rows, rows)
-    low = lambda dq: pl.ds(dq * rows, half)
-    high = lambda dq: pl.ds(dq * rows + half, half)
+    def whole(dq, i=0):
+        return pl.ds(dq * rows, NEAR if i == 5 else rows)
+
+    def low(dq, i=0):
+        return pl.ds(dq * rows, NEAR // 2 if i == 5 else half)
+
+    def high(dq, i=0):
+        return pl.ds(dq * rows + NEAR // 2, NEAR // 2) if i == 5 else pl.ds(dq * rows + half, half)
+
+    def far(dq):
+        return pl.ds(dq * rows + NEAR, rows - NEAR)
+
+    def prefix(i, n):
+        return pl.ds(0, n * NEAR // rows if i == 5 else n)
 
     def gather_q(i):
-        a = send(head.at[i, whole(0)], head.at[i, whole(3)], gq_s.at[i, 0], gq_r.at[i, 0], q_up)
-        b = send(head.at[i, whole(0)], head.at[i, whole(1)], gq_s.at[i, 1], gq_r.at[i, 1], q_down)
+        a = send(head.at[i, whole(0, i)], head.at[i, whole(3, i)], gq_s.at[i, 0], gq_r.at[i, 0], q_up)
+        b = send(head.at[i, whole(0, i)], head.at[i, whole(1, i)], gq_s.at[i, 1], gq_r.at[i, 1], q_down)
         return a, b
 
     def forward_q(i, pair):
         pair[0].wait_recv()
-        a = send(head.at[i, low(3)], head.at[i, low(2)], gq_s.at[i, 2], gq_r.at[i, 2], q_up)
+        a = send(head.at[i, low(3, i)], head.at[i, low(2, i)], gq_s.at[i, 2], gq_r.at[i, 2], q_up)
         pair[1].wait_recv()
-        b = send(head.at[i, high(1)], head.at[i, high(2)], gq_s.at[i, 3], gq_r.at[i, 3], q_down)
+        b = send(head.at[i, high(1, i)], head.at[i, high(2, i)], gq_s.at[i, 3], gq_r.at[i, 3], q_down)
         return a, b
 
     def gather_x(dp):
-        return send(head.at[2 * dp, whole(0)], head.at[2 * dp + 1, whole(0)], gx_s.at[dp], gx_r.at[dp], x_other)
+        i = 2 * dp
+        return send(head.at[i, whole(0, i + 1)], head.at[i + 1, whole(0, i + 1)], gx_s.at[dp], gx_r.at[dp], x_other)
+
+    def gather_far(dq):
+        return send(head.at[4, far(dq)], head.at[5, far(dq)], gf_s.at[dq], gf_r.at[dq], x_other)
 
     def norm_chunk(c, slot):
         xf = tok[slot].astype(F32)
@@ -127,9 +143,11 @@
             if c + slots < chunks:
                 token_copy(c + slots).start()
 
-    tile = 256
-
-    def add_logits(i, fresh):
+    def add_logits(i, fresh, tile=512):
+        if tile == vocab:
+            logits_t[...] += dot(head[i], normed_t[i], 0, 0)
+            return
+
         def step(j, carry):
             s = pl.ds(pl.multiple_of(j * tile, tile), tile)
             term = dot(head[i, :, s], normed_t[i], 0, 0)
@@ -141,11 +159,15 @@
 
         lax.fori_loop(0, vocab // tile, step, 0)
 
+    def finish(i, fresh=False, tile=512):
+        fq[i][0].wait_recv()
+        fq[i][1].wait_recv()
+        add_logits(i, fresh, tile)
+
     own = head.at[0, whole(0)]
     up = send(own, head.at[6, whole(0)], gp_s.at[0], gp_r.at[0], p_up)
     down = send(own, head.at[2, whole(0)], gp_s.at[1], gp_r.at[1], p_down)
-    gx = {0: gather_x(0)}
-    gq, fq = {0: gather_q(0)}, {}
+    gx, gq, fq, gf = {0: gather_x(0)}, {0: gather_q(0)}, {}, {}
     norm(0, 4)
     up.wait_recv()
     up2 = send(head.at[6, low(0)], head.at[4, low(0)], gp_s.at[2], gp_r.at[2], p_up)
@@ -155,42 +177,44 @@
     gx[3] = gather_x(3)
     gq[2] = gather_q(2)
     gq[6] = gather_q(6)
-    gx[0].wait_recv()
-    gq[1] = gather_q(1)
     norm(4, 6)
     fq[0] = forward_q(0, gq[0])
     up2.wait_recv()
     down2.wait_recv()
+    gq[4] = gather_q(4)
     gx[2] = gather_x(2)
-    gq[4] = gather_q(4)
+    gf[0] = gather_far(0)
+    gx[0].wait_recv()
+    gq[1] = gather_q(1)
     norm(6, 8)
     fq[2] = forward_q(2, gq[2])
     fq[6] = forward_q(6, gq[6])
-
-    def finish(i, fresh=False):
-        fq[i][0].wait_recv()
-        fq[i][1].wait_recv()
-        add_logits(i, fresh)
-
     finish(0, True)
+    fq[4] = forward_q(4, gq[4])
+    gf[1] = gather_far(1)
+    gf[3] = gather_far(3)
     gx[1].wait_recv()
     gq[3] = gather_q(3)
+    finish(2)
+    fq[4][0].wait_recv()
+    fq[4][1].wait_recv()
+    gf[2] = gather_far(2)
     gx[3].wait_recv()
     gq[7] = gather_q(7)
     fq[1] = forward_q(1, gq[1])
-    finish(2)
+    finish(6)
     gx[2].wait_recv()
     gq[5] = gather_q(5)
-    fq[4] = forward_q(4, gq[4])
-    finish(6)
+    add_logits(4, False)
     fq[3] = forward_q(3, gq[3])
     finish(1)
     fq[7] = forward_q(7, gq[7])
-    finish(4)
     fq[5] = forward_q(5, gq[5])
     finish(3)
+    for dq in (0, 1, 3, 2):
+        gf[dq].wait_recv()
     finish(7)
-    finish(5)
+    finish(5, tile=vocab)
 
     lanes = 128
 
@@ -207,17 +231,9 @@
 
     lax.fori_loop(0, count // lanes, soften, 0)
 
-    def term(i, dq):
-        grad[i, whole(dq)] = (dot(normed_t[i, whole(dq)], err_t[...], 1, 1) * scale).astype(BF16)
-
-    def start_terms(i):
-        term(i, 2)
-        a = send(grad.at[i, low(2)], rq_half.at[i, 0], sq_s.at[i, 0], sq_r.at[i, 0], q_up)
-        b = send(grad.at[i, high(2)], rq_half.at[i, 1], sq_s.at[i, 1], sq_r.at[i, 1], q_down)
-        term(i, 1)
-        term(i, 3)
-        term(i, 0)
-        return a, b
+    def terms(i, dq):
+        two = pl.ds(dq * rows, 2 * rows)
+        grad[i, two] = (dot(normed_t[i, two], err_t[...], 1, 1) * scale).astype(BF16)
 
     def add_into(i, where, *others):
         total = grad[i, where].astype(F32)
@@ -225,13 +241,35 @@
             total = total + other[...].astype(F32)
         grad[i, where] = total.astype(BF16)
 
+    sf = {}
+
+    def take_far(i, *slots_):
+        for dq in slots_ if i == 4 else ():
+            sf[dq].wait_recv()
+            add_into(4, far(dq), rx_far.at[dq])
+
+    def give_far(i, *slots_):
+        for dq in slots_ if i == 5 else ():
+            sf[dq] = send(grad.at[5, far(dq)], rx_far.at[dq], sf_s.at[dq], sf_r.at[dq], x_other)
+
+    def start_terms(i):
+        terms(i, 2)
+        take_far(i, 2)
+        a = send(grad.at[i, low(2, i)], rq_half.at[i, 0, prefix(i, half)], sq_s.at[i, 0], sq_r.at[i, 0], q_up)
+        b = send(grad.at[i, high(2, i)], rq_half.at[i, 1, prefix(i, half)], sq_s.at[i, 1], sq_r.at[i, 1], q_down)
+        give_far(i, 2, 3)
+        terms(i, 0)
+        give_far(i, 1, 0)
+        return a, b
+
     def pass_on(i, pair):
+        take_far(i, 1, 3)
         pair[0].wait_recv()
-        add_into(i, low(1), rq_half.at[i, 0])
-        a = send(grad.at[i, whole(1)], rq.at[i, 0], sq_s.at[i, 2], sq_r.at[i, 2], q_up)
+        add_into(i, low(1, i), rq_half.at[i, 0, prefix(i, half)])
+        a = send(grad.at[i, whole(1, i)], rq.at[i, 0, prefix(i, rows)], sq_s.at[i, 2], sq_r.at[i, 2], q_up)
         pair[1].wait_recv()
-        add_into(i, high(3), rq_half.at[i, 1])
-        b = send(grad.at[i, whole(3)], rq.at[i, 1], sq_s.at[i, 3], sq_r.at[i, 3], q_down)
+        add_into(i, high(3, i), rq_half.at[i, 1, prefix(i, half)])
+        b = send(grad.at[i, whole(3, i)], rq.at[i, 1, prefix(i, rows)], sq_s.at[i, 3], sq_r.at[i, 3], q_down)
         return a, b
 
     halves, wholes, sx = {}, {}, {}
@@ -242,11 +280,14 @@
             copy.wait_recv()
         dp, dx = i // 2, i % 2
         if dx:
+            n = prefix(i, rows)
+            add_into(i, whole(0, i), rq.at[i, 0, n], rq.at[i, 1, n])
+            sx[dp] = send(grad.at[i, whole(0, i)], rx.at[dp, n], sx_s.at[dp], sx_r.at[dp], x_other)
+        elif dp == 2:
+            take_far(4, 0)
+            sx[2].wait_recv()
             add_into(i, whole(0), rq.at[i, 0], rq.at[i, 1])
-            sx[dp] = send(grad.at[i, whole(0)], rx.at[dp], sx_s.at[dp], sx_r.at[dp], x_other)
-        elif dp == 2:
-            sx[2].wait_recv()
-            add_into(i, whole(0), rq.at[i, 0], rq.at[i, 1], rx.at[2])
+            add_into(i, whole(0, 5), rx.at[2, prefix(5, rows)])
             p_half.append(send(grad.at[i, low(0)], rp_half.at[0], sp_s.at[0], sp_r.at[0], p_up))
             p_half.append(send(grad.at[i, high(0)], rp_half.at[1], sp_s.at[1], sp_r.at[1], p_down))
         elif dp:
@@ -306,24 +347,32 @@
         summed = summed + rows_in[j]
     delta = held - summed[:run] / 4
     moment = 0.9 * moment + delta
+    moment_out[...] = moment
     fresh_rows = held - 0.7 * (delta + 0.9 * moment)
     new_out[pl.ds(0, run)] = fresh_rows
     new_out[pl.ds(run, pad - run)] = jnp.zeros((pad - run, part), F32)
     spread = [send(new_out, new_in.at[j], n_s.at[j], n_r.at[j], to) for j, to in enumerate(siblings)]
+    fresh_out[:, pl.ds(pl.multiple_of(r * part, part), part)] = fresh_rows
+    stepped_out[...] = stepped[pl.ds(0, rows)]
+    for j, copy in enumerate(spread):
+        copy.wait_recv()
+        fresh_out[:, pl.ds(pl.multiple_of(siblings[j][0] * part, part), part)] = new_in[j, pl.ds(0, run)]
+    for copy in sent:
+        copy.wait_send()
+
+
+def merge(loss, stepped, fresh, moment, momentum, step_index, frag_table, loss_out, weights_out, momentum_out):
+    frag_count = frag_table.shape[0]
+    run = fresh.shape[0]
+    pos = step_index[0] % frag_count
+    frag = jnp.int32(0)
+    for k in range(frag_count):
+        frag = frag + jnp.where(pos == k, frag_table[k], 0)
+    loss_out[...] = loss[...]
     for k in range(frag_count):
         s = pl.ds(k * run, run)
-        momentum_out[s] = jnp.where(frag == k, moment, momentum[s])
-        weights_out[s, pl.ds(pl.multiple_of(r * part, part), part)] = jnp.where(
-            frag == k, fresh_rows, stepped[s, pl.ds(pl.multiple_of(r * part, part), part)]
-        )
-    for j, copy in enumerate(spread):
-        copy.wait_recv()
-        columns = pl.ds(pl.multiple_of(siblings[j][0] * part, part), part)
-        for k in range(frag_count):
-            s = pl.ds(k * run, run)
-            weights_out[s, columns] = jnp.where(frag == k, new_in[j, pl.ds(0, run)], stepped[s, columns])
-    for copy in sent:
-        copy.wait_send()
+        weights_out[s] = jnp.where(frag == k, fresh[...], stepped[s])
+        momentum_out[s] = jnp.where(frag == k, moment[...], momentum[s])
 
 
 def on_device(tokens, targets, norm_gain, weights, anchor, momentum, step_index, frag_table):
@@ -337,15 +386,16 @@
     smem = pl.BlockSpec(memory_space=pltpu.SMEM)
     dma = pltpu.SemaphoreType.DMA
     big = pltpu.VMEM((8, 4 * rows, vocab), BF16)
-    loss, weights_out, momentum_out = pl.pallas_call(
+    shapes = (
+        jax.ShapeDtypeStruct((1, count), F32),
+        jax.ShapeDtypeStruct((rows, vocab), F32),
+        jax.ShapeDtypeStruct((rows, part), F32),
+    )
+    loss, stepped, fresh, moment = pl.pallas_call(
         kernel,
-        out_shape=(
-            jax.ShapeDtypeStruct((1, count), F32),
-            jax.ShapeDtypeStruct((rows, vocab), F32),
-            jax.ShapeDtypeStruct((rows, part), F32),
-        ),
+        out_shape=shapes[:2] + (jax.ShapeDtypeStruct((run, vocab), F32), jax.ShapeDtypeStruct((run, part), F32)),
         in_specs=[pl.BlockSpec(memory_space=pl.ANY)] + [vmem] * 5 + [smem] * 2,
-        out_specs=(vmem, vmem, vmem),
+        out_specs=(vmem,) * 4,
         scratch_shapes=[
             big,
             pltpu.VMEM((8, 4 * rows, count), BF16),
@@ -356,6 +406,7 @@
             pltpu.VMEM((8, 2, half, vocab), BF16),
             pltpu.VMEM((8, 2, rows, vocab), BF16),
             pltpu.VMEM((4, rows, vocab), BF16),
+            pltpu.VMEM((4, rows - NEAR, vocab), BF16),
             pltpu.VMEM((2, half, vocab), BF16),
             pltpu.VMEM((2, rows, vocab), BF16),
             pltpu.VMEM((rows + 8, vocab), F32),
@@ -364,8 +415,8 @@
             pltpu.VMEM((pad, part), F32),
             pltpu.VMEM((3, pad, part), F32),
             dma((4,)),
-            dma((4,)), dma((4,)), dma((4,)), dma((4,)), dma((8, 4)), dma((8, 4)),
-            dma((4,)), dma((4,)), dma((4,)), dma((4,)), dma((8, 4)), dma((8, 4)),
+            dma((4,)), dma((4,)), dma((4,)), dma((4,)), dma((4,)), dma((4,)), dma((8, 4)), dma((8, 4)),
+            dma((4,)), dma((4,)), dma((4,)), dma((4,)), dma((4,)), dma((4,)), dma((8, 4)), dma((8, 4)),
             dma((3,)), dma((3,)), dma((3,)), dma((3,)),
         ],
         compiler_params=pltpu.CompilerParams(
@@ -374,6 +425,9 @@
     )(
         tokens, targets, norm_gain[None], weights[0], anchor, momentum, step_index, frag_table
     )
+    loss, weights_out, momentum_out = pl.pallas_call(
+        merge, out_shape=shapes, in_specs=[vmem] * 5 + [smem] * 2, out_specs=(vmem,) * 3
+    )(loss, stepped, fresh, moment, momentum, step_index, frag_table)
     return (loss, weights_out[None], momentum_out)
 
 

time: 136 us -> 128 us (0.941)
  local copies, waits for them, and re-layouts: 4.84 us -> 0 us
  Pallas kernels: 130 us -> 127 us
    unnamed x3 -> x0, local copies, waits for them, and re-layouts: 4.84 us -> none
    pallas_call x1 -> x2, Pallas kernels: 130 us -> 127 us  [the longest x1 125 us: on_device(): pl.pallas_call(kernel, out_shape=shapes[:2] + (jax.ShapeDtypeStruct((run,...]
where the time goes in v2:
time: 128 us
  Pallas kernels  127 us (99%)
  between operations  1.29 us (1%)
    pallas_call x1, Pallas kernels, on_device(): pl.pallas_call(kernel, out_shape=shapes[:2] + (jax.ShapeDtypeStruct((run,...  125 us

profile of v2, /device:TPU:1, one launch (start us, length us, event | category | flops | bytes accessed | tf_op | source)
XLA Modules:
  0.0 128.1 jit_solution(7121124592108550168)
XLA Ops:
  1.3 124.7 %shard_map.103 = (f32[1,1024]{1,0:T(1,128)}, f32[160,1024]{1,0:T(8,128)}, f32[20,1024]{1,0:T(8,128)}, f32[20,256]{1,0:T(8,128)}) custom-call(bf16[1,1024,5120]{2,1,0:T(8,128)(2,1)} %tokens.1, s32[1,1024]{1,0:T(1,128)} %targets.1, f32[1,5120]{1,0:T(1,128)} %bitcast.4, f32[160,1024]{1,0:T(8,128)} %bitcast.3, f32[160,256]{1,0:T(8,128)} %anchor.1, ...), custom_call_target="tpu_custom_call" | custom-call | tf_op jit(solution)/shard_map/pallas_call | solution.py:394
  125.9 2.1 %shard_map.104 = (f32[1,1024]{1,0:T(1,128)}, f32[160,1024]{1,0:T(8,128)}, f32[160,256]{1,0:T(8,128)}) custom-call(f32[1,1024]{1,0:T(1,128)} %get-tuple-element.10.loss, f32[160,1024]{1,0:T(8,128)} %get-tuple-element.11.stepped, f32[20,1024]{1,0:T(8,128)} %get-tuple-element.12.fresh, f32[20,256]{1,0:T(8,128)} %get-tuple-element.13.moment, ...), custom_call_target="tpu_custom_call" | custom-call | tf_op jit(solution)/shard_map/pallas_call | solution.py:428

commit v3 on v2

--- a/solution.py
+++ b/solution.py
@@ -13,6 +13,7 @@
 MESH = pl.DeviceIdType.MESH
 
 SCATTER_ORDER = (5, 7, 3, 1, 4, 6, 2, 0)
+SLOT = (0, 1, 3, 2)
 NEAR = 64
 
 
@@ -82,16 +83,17 @@
         return copy
 
     def whole(dq, i=0):
-        return pl.ds(dq * rows, NEAR if i == 5 else rows)
+        return pl.ds(SLOT[dq] * rows, NEAR if i == 5 else rows)
 
     def low(dq, i=0):
-        return pl.ds(dq * rows, NEAR // 2 if i == 5 else half)
+        return pl.ds(SLOT[dq] * rows, NEAR // 2 if i == 5 else half)
 
     def high(dq, i=0):
-        return pl.ds(dq * rows + NEAR // 2, NEAR // 2) if i == 5 else pl.ds(dq * rows + half, half)
+        cut = NEAR // 2 if i == 5 else half
+        return pl.ds(SLOT[dq] * rows + cut, cut)
 
     def far(dq):
-        return pl.ds(dq * rows + NEAR, rows - NEAR)
+        return pl.ds(SLOT[dq] * rows + NEAR, rows - NEAR)
 
     def prefix(i, n):
         return pl.ds(0, n * NEAR // rows if i == 5 else n)
@@ -129,7 +131,7 @@
                 dx = (bx + x) % 2
                 normed_t[
                     2 * dp + dx,
-                    pl.ds(pl.multiple_of(dq * rows, 16), rows),
+                    pl.ds(pl.multiple_of((dq ^ (dq >> 1)) * rows, 16), rows),
                     pl.ds(pl.multiple_of(c * chunk, chunk), chunk),
                 ] = part[b * rows : (b + 1) * rows]
             return carry
@@ -143,14 +145,15 @@
             if c + slots < chunks:
                 token_copy(c + slots).start()
 
-    def add_logits(i, fresh, tile=512):
-        if tile == vocab:
-            logits_t[...] += dot(head[i], normed_t[i], 0, 0)
-            return
+    early = pl.ds(0, 3 * rows)
+    last = pl.ds(3 * rows, rows)
+
+    def add_logits(i, where=pl.ds(0, 4 * rows), fresh=False):
+        tile = vocab // 2
 
         def step(j, carry):
             s = pl.ds(pl.multiple_of(j * tile, tile), tile)
-            term = dot(head[i, :, s], normed_t[i], 0, 0)
+            term = dot(head[i, where, s], normed_t[i, where], 0, 0)
             if fresh:
                 logits_t[s, :] = term
             else:
@@ -159,10 +162,13 @@
 
         lax.fori_loop(0, vocab // tile, step, 0)
 
-    def finish(i, fresh=False, tile=512):
+    def settle_q(i):
         fq[i][0].wait_recv()
         fq[i][1].wait_recv()
-        add_logits(i, fresh, tile)
+
+    def finish(i, fresh=False):
+        settle_q(i)
+        add_logits(i, fresh=fresh)
 
     own = head.at[0, whole(0)]
     up = send(own, head.at[6, whole(0)], gp_s.at[0], gp_r.at[0], p_up)
@@ -189,7 +195,7 @@
     norm(6, 8)
     fq[2] = forward_q(2, gq[2])
     fq[6] = forward_q(6, gq[6])
-    finish(0, True)
+    finish(0, fresh=True)
     fq[4] = forward_q(4, gq[4])
     gf[1] = gather_far(1)
     gf[3] = gather_far(3)
@@ -205,16 +211,23 @@
     finish(6)
     gx[2].wait_recv()
     gq[5] = gather_q(5)
-    add_logits(4, False)
     fq[3] = forward_q(3, gq[3])
+    add_logits(4)
+    fq[7] = forward_q(7, gq[7])
     finish(1)
-    fq[7] = forward_q(7, gq[7])
     fq[5] = forward_q(5, gq[5])
-    finish(3)
-    for dq in (0, 1, 3, 2):
+    add_logits(3, early)
+    add_logits(7, early)
+    for dq in (0, 1, 3):
         gf[dq].wait_recv()
-    finish(7)
-    finish(5, tile=vocab)
+    add_logits(5, early)
+    gf[2].wait_recv()
+    tail = (3, 7, 5)
+    for i in tail:
+        settle_q(i)
+    logits_t[...] += dot(
+        jnp.concatenate([head[i, last] for i in tail]), jnp.concatenate([normed_t[i, last] for i in tail]), 0, 0
+    )
 
     lanes = 128
 
@@ -231,8 +244,8 @@
 
     lax.fori_loop(0, count // lanes, soften, 0)
 
-    def terms(i, dq):
-        two = pl.ds(dq * rows, 2 * rows)
+    def terms(i, slot):
+        two = pl.ds(slot * rows, 2 * rows)
         grad[i, two] = (dot(normed_t[i, two], err_t[...], 1, 1) * scale).astype(BF16)
 
     def add_into(i, where, *others):

time: 128 us -> 125 us (0.977)
  Pallas kernels: 127 us -> 124 us
    pallas_call x1, Pallas kernels: 125 us -> 122 us  [on_device(): pl.pallas_call(kernel, out_shape=shapes[:2] + (jax.ShapeDtypeStruct((run,...]
where the time goes in v3:
time: 125 us
  Pallas kernels  124 us (99%)
  between operations  1.29 us (1%)
    pallas_call x1, Pallas kernels, on_device(): pl.pallas_call(kernel, out_shape=shapes[:2] + (jax.ShapeDtypeStruct((run,...  122 us

profile of v3, /device:TPU:1, one launch (start us, length us, event | category | flops | bytes accessed | tf_op | source)
XLA Modules:
  0.0 125.1 jit_solution(13345287899308661384)
XLA Ops:
  1.3 121.7 %shard_map.103 = (f32[1,1024]{1,0:T(1,128)}, f32[160,1024]{1,0:T(8,128)}, f32[20,1024]{1,0:T(8,128)}, f32[20,256]{1,0:T(8,128)}) custom-call(bf16[1,1024,5120]{2,1,0:T(8,128)(2,1)} %tokens.1, s32[1,1024]{1,0:T(1,128)} %targets.1, f32[1,5120]{1,0:T(1,128)} %bitcast.4, f32[160,1024]{1,0:T(8,128)} %bitcast.3, f32[160,256]{1,0:T(8,128)} %anchor.1, ...), custom_call_target="tpu_custom_call" | custom-call | tf_op jit(solution)/shard_map/pallas_call | solution.py:407
  123.0 2.1 %shard_map.104 = (f32[1,1024]{1,0:T(1,128)}, f32[160,1024]{1,0:T(8,128)}, f32[160,256]{1,0:T(8,128)}) custom-call(f32[1,1024]{1,0:T(1,128)} %get-tuple-element.10.loss, f32[160,1024]{1,0:T(8,128)} %get-tuple-element.11.stepped, f32[20,1024]{1,0:T(8,128)} %get-tuple-element.12.fresh, f32[20,256]{1,0:T(8,128)} %get-tuple-element.13.moment, ...), custom_call_target="tpu_custom_call" | custom-call | tf_op jit(solution)/shard_map/pallas_call | solution.py:441

commit v4 on v3

--- a/solution.py
+++ b/solution.py
@@ -13,6 +13,8 @@
 MESH = pl.DeviceIdType.MESH
 
 SCATTER_ORDER = (5, 7, 3, 1, 4, 6, 2, 0)
+FIRST = 32
+ROLL = (16, 40, 80)
 SLOT = (0, 1, 3, 2)
 NEAR = 64
 
@@ -24,7 +26,7 @@
 def kernel(
     tokens, targets, gain, weights, anchor, momentum, step_index, frag_table,
     loss_out, stepped_out, fresh_out, moment_out,
-    head, normed_t, grad, logits_t, err_t, tok, rq_half, rq, rx, rx_far, rp_half, rp, stepped, rows_out, rows_in, new_out, new_in,
+    head, normed_t, grad, logits_t, err_t, tok, rq_half, rq, rx, rx_far, rp_half, rp, rolled, rows_out, rows_in, new_out, new_in,
     tok_sem, gp_s, gp_r, gx_s, gx_r, gf_s, gf_r, gq_s, gq_r,
     sp_s, sp_r, sx_s, sx_r, sf_s, sf_r, sq_s, sq_r, e_s, e_r, n_s, n_r,
 ):
@@ -69,7 +71,19 @@
 
     for c in range(slots):
         token_copy(c).start()
-    head[0, pl.ds(0, rows)] = weights[...].astype(BF16)
+    pos = step_index[0] % frag_count
+    frag = jnp.int32(0)
+    for k in range(frag_count):
+        frag = frag + jnp.where(pos == k, frag_table[k], 0)
+    bits = [frag % 2 == 1, frag // 2 % 2 == 1, frag // 4 == 1]
+
+    def roll_up(value):
+        for bit, step in zip(bits, ROLL):
+            value = jnp.where(bit, jnp.concatenate([value[step:], value[:step]]), value)
+        return value
+
+    rolled[...] = roll_up(weights[...])
+    head[0, pl.ds(0, rows)] = rolled[...].astype(BF16)
     pl.semaphore_wait(barrier, len(partners))
 
     sent = []
@@ -95,9 +109,6 @@
     def far(dq):
         return pl.ds(SLOT[dq] * rows + NEAR, rows - NEAR)
 
-    def prefix(i, n):
-        return pl.ds(0, n * NEAR // rows if i == 5 else n)
-
     def gather_q(i):
         a = send(head.at[i, whole(0, i)], head.at[i, whole(3, i)], gq_s.at[i, 0], gq_r.at[i, 0], q_up)
         b = send(head.at[i, whole(0, i)], head.at[i, whole(1, i)], gq_s.at[i, 1], gq_r.at[i, 1], q_down)
@@ -123,7 +134,7 @@
 
         def unit(j, carry):
             columns = pl.ds(pl.multiple_of(j * 4 * rows, 128), 4 * rows)
-            part = (tok[slot, :, columns].astype(F32) * inv * gain[:, columns]).astype(BF16).T
+            part = (tok[slot, :, columns].astype(F32) * inv * gain[:, columns]).T
             for b in range(4):
                 bz, by, bx = j // 2, 2 * (j % 2) + b // 2, b % 2
                 dp = (jnp.where(core == 0, bz, by) - p + 4) % 4
@@ -133,7 +144,7 @@
                     2 * dp + dx,
                     pl.ds(pl.multiple_of((dq ^ (dq >> 1)) * rows, 16), rows),
                     pl.ds(pl.multiple_of(c * chunk, chunk), chunk),
-                ] = part[b * rows : (b + 1) * rows]
+                ] = roll_up(part[b * rows : (b + 1) * rows]).astype(BF16)
             return carry
 
         lax.fori_loop(0, width // (4 * rows), unit, 0)
@@ -254,138 +265,212 @@
             total = total + other[...].astype(F32)
         grad[i, where] = total.astype(BF16)
 
-    sf = {}
-
-    def take_far(i, *slots_):
-        for dq in slots_ if i == 4 else ():
-            sf[dq].wait_recv()
-            add_into(4, far(dq), rx_far.at[dq])
-
-    def give_far(i, *slots_):
-        for dq in slots_ if i == 5 else ():
-            sf[dq] = send(grad.at[5, far(dq)], rx_far.at[dq], sf_s.at[dq], sf_r.at[dq], x_other)
+    def near(part, i):
+        if i == 5:
+            return (0, 0) if part == 0 else (FIRST, NEAR)
+        return (0, FIRST) if part == 0 else (FIRST, rows - FIRST)
+
+    def beyond(part):
+        return (0, FIRST) if part == 0 else (FIRST + NEAR, rows - FIRST - NEAR)
+
+    def at(dq, span):
+        return pl.ds(SLOT[dq] * rows + span[0], span[1])
+
+    def bottom(span):
+        return span[0], span[1] // 2
+
+    def top(span):
+        return span[0] + span[1] // 2, span[1] // 2
+
+    def slot_half(part, i):
+        return pl.ds(0 if part == 0 else FIRST // 2, near(part, i)[1] // 2)
+
+    def slot_far(part):
+        return pl.ds(0 if part == 0 else FIRST, beyond(part)[1])
+
+    sf, sx, p_half, p_whole, halves, wholes = {}, {}, {}, {}, {}, {}
+
+    def take_far(i, part, *offsets):
+        for dq in offsets if i == 4 else ():
+            sf[part, dq].wait_recv()
+            add_into(4, at(dq, beyond(part)), rx_far.at[dq, slot_far(part)])
+
+    def give_far(i, part, *offsets):
+        for dq in offsets if i == 5 else ():
+            sf[part, dq] = send(
+                grad.at[5, at(dq, beyond(part))], rx_far.at[dq, slot_far(part)],
+                sf_s.at[part, dq], sf_r.at[part, dq], x_other,
+            )
+
+    def start_halves(i, part):
+        take_far(i, part, 2)
+        span = near(part, i)
+        if span[1]:
+            land = slot_half(part, i)
+            s_sem, r_sem = sq_s.at[part, i], sq_r.at[part, i]
+            halves[part, i] = (
+                send(grad.at[i, at(2, bottom(span))], rq_half.at[i, 0, land], s_sem.at[0], r_sem.at[0], q_up),
+                send(grad.at[i, at(2, top(span))], rq_half.at[i, 1, land], s_sem.at[1], r_sem.at[1], q_down),
+            )
 
     def start_terms(i):
         terms(i, 2)
-        take_far(i, 2)
-        a = send(grad.at[i, low(2, i)], rq_half.at[i, 0, prefix(i, half)], sq_s.at[i, 0], sq_r.at[i, 0], q_up)
-        b = send(grad.at[i, high(2, i)], rq_half.at[i, 1, prefix(i, half)], sq_s.at[i, 1], sq_r.at[i, 1], q_down)
-        give_far(i, 2, 3)
+        give_far(i, 0, 2, 3)
+        start_halves(i, 0)
+        give_far(i, 1, 2)
+        start_halves(i, 1)
         terms(i, 0)
-        give_far(i, 1, 0)
-        return a, b
-
-    def pass_on(i, pair):
-        take_far(i, 1, 3)
-        pair[0].wait_recv()
-        add_into(i, low(1, i), rq_half.at[i, 0, prefix(i, half)])
-        a = send(grad.at[i, whole(1, i)], rq.at[i, 0, prefix(i, rows)], sq_s.at[i, 2], sq_r.at[i, 2], q_up)
-        pair[1].wait_recv()
-        add_into(i, high(3, i), rq_half.at[i, 1, prefix(i, half)])
-        b = send(grad.at[i, whole(3, i)], rq.at[i, 1, prefix(i, rows)], sq_s.at[i, 3], sq_r.at[i, 3], q_down)
-        return a, b
-
-    halves, wholes, sx = {}, {}, {}
-    p_half, p_whole = [], {}
-
-    def settle(i):
-        for copy in wholes[i]:
+        give_far(i, 0, 1, 0)
+        give_far(i, 1, 3, 1, 0)
+
+    def pass_on(i, part):
+        take_far(i, part, 1, 3)
+        span = near(part, i)
+        if span[1]:
+            land, rest = slot_half(part, i), pl.ds(*span)
+            s_sem, r_sem = sq_s.at[part, i], sq_r.at[part, i]
+            up, down = halves[part, i]
+            up.wait_recv()
+            add_into(i, at(1, bottom(span)), rq_half.at[i, 0, land])
+            a = send(grad.at[i, at(1, span)], rq.at[i, 0, rest], s_sem.at[2], r_sem.at[2], q_up)
+            down.wait_recv()
+            add_into(i, at(3, top(span)), rq_half.at[i, 1, land])
+            b = send(grad.at[i, at(3, span)], rq.at[i, 1, rest], s_sem.at[3], r_sem.at[3], q_down)
+            wholes[part, i] = a, b
+
+    def settle(i, part):
+        span = near(part, i)
+        if not span[1]:
+            return
+        for copy in wholes[part, i]:
             copy.wait_recv()
         dp, dx = i // 2, i % 2
+        rest = pl.ds(*span)
+        own = at(0, span)
+        land = slot_half(part, i)
+        up, down = p_up, p_down
         if dx:
-            n = prefix(i, rows)
-            add_into(i, whole(0, i), rq.at[i, 0, n], rq.at[i, 1, n])
-            sx[dp] = send(grad.at[i, whole(0, i)], rx.at[dp, n], sx_s.at[dp], sx_r.at[dp], x_other)
+            add_into(i, own, rq.at[i, 0, rest], rq.at[i, 1, rest])
+            sx[part, dp] = send(
+                grad.at[i, own], rx.at[dp, rest], sx_s.at[part, dp], sx_r.at[part, dp], x_other
+            )
         elif dp == 2:
-            take_far(4, 0)
-            sx[2].wait_recv()
-            add_into(i, whole(0), rq.at[i, 0], rq.at[i, 1])
-            add_into(i, whole(0, 5), rx.at[2, prefix(5, rows)])
-            p_half.append(send(grad.at[i, low(0)], rp_half.at[0], sp_s.at[0], sp_r.at[0], p_up))
-            p_half.append(send(grad.at[i, high(0)], rp_half.at[1], sp_s.at[1], sp_r.at[1], p_down))
+            take_far(4, part, 0)
+            add_into(i, own, rq.at[i, 0, rest], rq.at[i, 1, rest])
+            crossed = near(part, 5)
+            if crossed[1]:
+                sx[part, 2].wait_recv()
+                add_into(i, at(0, crossed), rx.at[2, pl.ds(*crossed)])
+            p_half[part, 0] = send(
+                grad.at[i, at(0, bottom(span))], rp_half.at[0, land], sp_s.at[part, 0], sp_r.at[part, 0], up
+            )
+            p_half[part, 1] = send(
+                grad.at[i, at(0, top(span))], rp_half.at[1, land], sp_s.at[part, 1], sp_r.at[part, 1], down
+            )
         elif dp:
-            sx[dp].wait_recv()
-            add_into(i, whole(0), rq.at[i, 0], rq.at[i, 1], rx.at[dp])
-            if dp == 1:
-                p_half[0].wait_recv()
-                add_into(i, low(0), rp_half.at[0])
-                p_whole[0] = send(grad.at[i, whole(0)], rp.at[0], sp_s.at[2], sp_r.at[2], p_up)
-            else:
-                p_half[1].wait_recv()
-                add_into(i, high(0), rp_half.at[1])
-                p_whole[1] = send(grad.at[i, whole(0)], rp.at[1], sp_s.at[3], sp_r.at[3], p_down)
+            sx[part, dp].wait_recv()
+            add_into(i, own, rq.at[i, 0, rest], rq.at[i, 1, rest], rx.at[dp, rest])
+            k = dp // 2
+            p_half[part, k].wait_recv()
+            add_into(i, at(0, (bottom, top)[k](span)), rp_half.at[k, land])
+            p_whole[part, k] = send(
+                grad.at[i, own], rp.at[k, rest], sp_s.at[part, 2 + k], sp_r.at[part, 2 + k], (up, down)[k]
+            )
+
+    def step_rows(part):
+        span = near(part, 0)
+        rest = pl.ds(*span)
+        for copy in wholes[part, 0]:
+            copy.wait_recv()
+        sx[part, 0].wait_recv()
+        total = grad[0, at(0, span)].astype(F32)
+        for term in (rq.at[0, 0], rq.at[0, 1], rx.at[0]):
+            total = total + term[rest].astype(F32)
+        for k in (1, 0):
+            p_whole[part, k].wait_recv()
+            total = total + rp[k, rest].astype(F32)
+        stepped_out[rest] = rolled[rest] - total
+
+    pad = rows_out.shape[1]
+    part_width = vocab // 4
+    exchange, spread = [], []
+
+    def my_columns(who):
+        return pl.ds(pl.multiple_of(who * part_width, part_width), part_width)
+
+    def start_sync():
+        step_rows(0)
+        for k in range(4):
+            rows_out[k] = stepped_out[pl.ds(0, pad), k * part_width : (k + 1) * part_width]
+        for j, to in enumerate(siblings):
+            exchange.append(send(rows_out.at[to[0]], rows_in.at[j], e_s.at[j], e_r.at[j], to))
+
+    def turn_sync():
+        held = roll_up(anchor[...])[:pad]
+        summed = rows_out[r]
+        for j, copy in enumerate(exchange):
+            copy.wait_recv()
+            summed = summed + rows_in[j]
+        delta = held - summed / 4
+        moment = 0.9 * roll_up(momentum[...])[:pad] + delta
+        moment_out[...] = moment
+        fresh_rows = held - 0.7 * (delta + 0.9 * moment)
+        new_out[...] = fresh_rows
+        for j, to in enumerate(siblings):
+            spread.append(send(new_out, new_in.at[j], n_s.at[j], n_r.at[j], to))
+        fresh_out[:, my_columns(r)] = fresh_rows
+
+    def end_sync():
+        for j, copy in enumerate(spread):
+            copy.wait_recv()
+            fresh_out[:, my_columns(siblings[j][0])] = new_in[j]
 
     order = SCATTER_ORDER
-    halves[order[0]] = start_terms(order[0])
+    start_terms(order[0])
     for k, i in enumerate(order):
         if k + 1 < len(order):
-            halves[order[k + 1]] = start_terms(order[k + 1])
-        wholes[i] = pass_on(i, halves[i])
+            start_terms(order[k + 1])
+        pass_on(i, 0)
         if k:
-            settle(order[k - 1])
-    for copy in wholes[0]:
-        copy.wait_recv()
-    sx[0].wait_recv()
-    total = grad[0, whole(0)].astype(F32)
-    for part in (rq.at[0, 0], rq.at[0, 1], rx.at[0]):
-        total = total + part[...].astype(F32)
-    for k in (1, 0):
-        p_whole[k].wait_recv()
-        total = total + rp[k].astype(F32)
-    stepped[pl.ds(0, rows)] = weights[...] - total
-    stepped[pl.ds(rows, 8)] = jnp.zeros((8, vocab), F32)
-
+            settle(order[k - 1], 0)
+    between = {2: start_sync, 4: turn_sync, 6: end_sync}
+    for k, i in enumerate(order):
+        pass_on(i, 1)
+        if k:
+            settle(order[k - 1], 1)
+        if k in between:
+            between[k]()
+    step_rows(1)
+    for copy in sent:
+        copy.wait_send()
+
+
+def merge(
+    loss, stepped, fresh, moment, momentum, step_index, frag_table, loss_out, weights_out, momentum_out, rolled
+):
+    frag_count = frag_table.shape[0]
+    rows = stepped.shape[0]
+    run = rows // frag_count
+    pad = fresh.shape[0]
     pos = step_index[0] % frag_count
     frag = jnp.int32(0)
     for k in range(frag_count):
         frag = frag + jnp.where(pos == k, frag_table[k], 0)
-    pad = rows_out.shape[1]
-    part = vocab // 4
-    mine = jnp.zeros((pad, vocab), F32)
-    for k in range(frag_count):
-        mine = jnp.where(frag == k, stepped[pl.ds(k * run, pad)], mine)
-    for k in range(4):
-        rows_out[k] = mine[:, k * part : (k + 1) * part]
-    exchange = [
-        send(rows_out.at[to[0]], rows_in.at[j], e_s.at[j], e_r.at[j], to) for j, to in enumerate(siblings)
-    ]
-    held = jnp.zeros((run, part), F32)
-    moment = jnp.zeros((run, part), F32)
-    for k in range(frag_count):
-        held = jnp.where(frag == k, anchor[pl.ds(k * run, run)], held)
-        moment = jnp.where(frag == k, momentum[pl.ds(k * run, run)], moment)
-    summed = rows_out[r]
-    for j, copy in enumerate(exchange):
-        copy.wait_recv()
-        summed = summed + rows_in[j]
-    delta = held - summed[:run] / 4
-    moment = 0.9 * moment + delta
-    moment_out[...] = moment
-    fresh_rows = held - 0.7 * (delta + 0.9 * moment)
-    new_out[pl.ds(0, run)] = fresh_rows
-    new_out[pl.ds(run, pad - run)] = jnp.zeros((pad - run, part), F32)
-    spread = [send(new_out, new_in.at[j], n_s.at[j], n_r.at[j], to) for j, to in enumerate(siblings)]
-    fresh_out[:, pl.ds(pl.multiple_of(r * part, part), part)] = fresh_rows
-    stepped_out[...] = stepped[pl.ds(0, rows)]
-    for j, copy in enumerate(spread):
-        copy.wait_recv()
-        fresh_out[:, pl.ds(pl.multiple_of(siblings[j][0] * part, part), part)] = new_in[j, pl.ds(0, run)]
-    for copy in sent:
-        copy.wait_send()
-
-
-def merge(loss, stepped, fresh, moment, momentum, step_index, frag_table, loss_out, weights_out, momentum_out):
-    frag_count = frag_table.shape[0]
-    run = fresh.shape[0]
-    pos = step_index[0] % frag_count
-    frag = jnp.int32(0)
-    for k in range(frag_count):
-        frag = frag + jnp.where(pos == k, frag_table[k], 0)
+    offset = pl.multiple_of(frag * run // 8 * 8, 8)
+    skip = frag * run - offset
+
+    def synced(shape):
+        row = lax.broadcasted_iota(jnp.int32, shape, 0)
+        return (row >= skip) & (row < skip + run)
+
     loss_out[...] = loss[...]
-    for k in range(frag_count):
-        s = pl.ds(k * run, run)
-        weights_out[s] = jnp.where(frag == k, fresh[...], stepped[s])
-        momentum_out[s] = jnp.where(frag == k, moment[...], momentum[s])
+    mixed = jnp.where(synced(fresh.shape), fresh[...], stepped[pl.ds(0, pad)])
+    for k in range(2):
+        rolled[pl.ds(k * rows, pad)] = mixed
+        rolled[pl.ds(k * rows + pad, rows - pad)] = stepped[pl.ds(pad, rows - pad)]
+    weights_out[...] = rolled[pl.ds(pl.multiple_of((rows - offset) % rows, 8), rows)]
+    momentum_out[...] = momentum[...]
+    momentum_out[pl.ds(offset, pad)] = jnp.where(synced(moment.shape), moment[...], momentum[pl.ds(offset, pad)])
 
 
 def on_device(tokens, targets, norm_gain, weights, anchor, momentum, step_index, frag_table):
@@ -406,7 +491,7 @@
     )
     loss, stepped, fresh, moment = pl.pallas_call(
         kernel,
-        out_shape=shapes[:2] + (jax.ShapeDtypeStruct((run, vocab), F32), jax.ShapeDtypeStruct((run, part), F32)),
+        out_shape=shapes[:2] + (jax.ShapeDtypeStruct((pad, vocab), F32), jax.ShapeDtypeStruct((pad, part), F32)),
         in_specs=[pl.BlockSpec(memory_space=pl.ANY)] + [vmem] * 5 + [smem] * 2,
         out_specs=(vmem,) * 4,
         scratch_shapes=[
@@ -415,21 +500,21 @@
             big,
             pltpu.VMEM((vocab, count), F32),
             pltpu.VMEM((vocab, count), BF16),
-            pltpu.VMEM((4, 128, width), BF16),
+            pltpu.VMEM((2, 128, width), BF16),
             pltpu.VMEM((8, 2, half, vocab), BF16),
             pltpu.VMEM((8, 2, rows, vocab), BF16),
             pltpu.VMEM((4, rows, vocab), BF16),
             pltpu.VMEM((4, rows - NEAR, vocab), BF16),
             pltpu.VMEM((2, half, vocab), BF16),
             pltpu.VMEM((2, rows, vocab), BF16),
-            pltpu.VMEM((rows + 8, vocab), F32),
+            pltpu.VMEM((rows, vocab), F32),
             pltpu.VMEM((4, pad, part), F32),
             pltpu.VMEM((3, pad, part), F32),
             pltpu.VMEM((pad, part), F32),
             pltpu.VMEM((3, pad, part), F32),
-            dma((4,)),
+            dma((2,)),
             dma((4,)), dma((4,)), dma((4,)), dma((4,)), dma((4,)), dma((4,)), dma((8, 4)), dma((8, 4)),
-            dma((4,)), dma((4,)), dma((4,)), dma((4,)), dma((4,)), dma((4,)), dma((8, 4)), dma((8, 4)),
+            dma((2, 4)), dma((2, 4)), dma((2, 4)), dma((2, 4)), dma((2, 4)), dma((2, 4)), dma((2, 8, 4)), dma((2, 8, 4)),
             dma((3,)), dma((3,)), dma((3,)), dma((3,)),
         ],
         compiler_params=pltpu.CompilerParams(
@@ -439,7 +524,8 @@
         tokens, targets, norm_gain[None], weights[0], anchor, momentum, step_index, frag_table
     )
     loss, weights_out, momentum_out = pl.pallas_call(
-        merge, out_shape=shapes, in_specs=[vmem] * 5 + [smem] * 2, out_specs=(vmem,) * 3
+        merge, out_shape=shapes, in_specs=[vmem] * 5 + [smem] * 2, out_specs=(vmem,) * 3,
+        scratch_shapes=[pltpu.VMEM((2 * rows, vocab), F32)],
     )(loss, stepped, fresh, moment, momentum, step_index, frag_table)
     return (loss, weights_out[None], momentum_out)
 

time: 125 us -> 131 us (1.048)
  Pallas kernels: 124 us -> 129 us
    pallas_call x1, Pallas kernels: 122 us -> 127 us  [on_device(): pl.pallas_call(kernel, out_shape=shapes[:2] + (jax.ShapeDtypeStruct((pad,...]
where the time goes in v4:
time: 131 us; the launch traced here: 130 us
  Pallas kernels  129 us (98%)
    pallas_call x1, Pallas kernels, on_device(): pl.pallas_call(kernel, out_shape=shapes[:2] + (jax.ShapeDtypeStruct((pad,...  127 us

profile of v4, /device:TPU:1, one launch (start us, length us, event | category | flops | bytes accessed | tf_op | source)
XLA Modules:
  0.0 130.4 jit_solution(14641853598307037676)
XLA Ops:
  1.3 126.9 %shard_map.103 = (f32[1,1024]{1,0:T(1,128)}, f32[160,1024]{1,0:T(8,128)}, f32[24,1024]{1,0:T(8,128)}, f32[24,256]{1,0:T(8,128)}) custom-call(bf16[1,1024,5120]{2,1,0:T(8,128)(2,1)} %tokens.1, s32[1,1024]{1,0:T(1,128)} %targets.1, f32[1,5120]{1,0:T(1,128)} %bitcast.4, f32[160,1024]{1,0:T(8,128)} %bitcast.3, f32[160,256]{1,0:T(8,128)} %anchor.1, ...), custom_call_target="tpu_custom_call" | custom-call | tf_op jit(solution)/shard_map/pallas_call | solution.py:492
  128.2 2.2 %shard_map.104 = (f32[1,1024]{1,0:T(1,128)}, f32[160,1024]{1,0:T(8,128)}, f32[160,256]{1,0:T(8,128)}) custom-call(f32[1,1024]{1,0:T(1,128)} %get-tuple-element.10.loss, f32[160,1024]{1,0:T(8,128)} %get-tuple-element.11.stepped, f32[24,1024]{1,0:T(8,128)} %get-tuple-element.12.fresh, f32[24,256]{1,0:T(8,128)} %get-tuple-element.13.moment, ...), custom_call_target="tpu_custom_call" | custom-call | tf_op jit(solution)/shard_map/pallas_call | solution.py:526

commit v5 on v4

--- a/solution.py
+++ b/solution.py
@@ -12,7 +12,14 @@
 BF16 = jnp.bfloat16
 MESH = pl.DeviceIdType.MESH
 
-SCATTER_ORDER = (5, 7, 3, 1, 4, 6, 2, 0)
+PLAN = (
+    "T7", "h7", "T3", "P7", "h3", "T5", "h5", "p7",
+    "T1", "p5", "h1", "T2", "h2", "T4", "p3", "T6",
+    "P1", "T0", "P3", "S7", "P4", "h6", "P6", "S1",
+    "h0", "P0", "S4", "s5", "P2", "p1", "h4", "S6",
+    "S3", "s3", "p6", "S2", "s7", "p4", "X0", "p2",
+    "s4", "s1", "p0", "X1", "s2", "s6", "X2",
+)
 FIRST = 32
 ROLL = (16, 40, 80)
 SLOT = (0, 1, 3, 2)
@@ -317,10 +324,12 @@
         terms(i, 2)
         give_far(i, 0, 2, 3)
         start_halves(i, 0)
+        terms(i, 0)
+        give_far(i, 0, 1, 0)
+
+    def start_rest(i):
         give_far(i, 1, 2)
         start_halves(i, 1)
-        terms(i, 0)
-        give_far(i, 0, 1, 0)
         give_far(i, 1, 3, 1, 0)
 
     def pass_on(i, part):
@@ -425,21 +434,17 @@
             copy.wait_recv()
             fresh_out[:, my_columns(siblings[j][0])] = new_in[j]
 
-    order = SCATTER_ORDER
-    start_terms(order[0])
-    for k, i in enumerate(order):
-        if k + 1 < len(order):
-            start_terms(order[k + 1])
-        pass_on(i, 0)
-        if k:
-            settle(order[k - 1], 0)
-    between = {2: start_sync, 4: turn_sync, 6: end_sync}
-    for k, i in enumerate(order):
-        pass_on(i, 1)
-        if k:
-            settle(order[k - 1], 1)
-        if k in between:
-            between[k]()
+    act = {
+        "T": start_terms,
+        "h": start_rest,
+        "P": lambda i: pass_on(i, 0),
+        "S": lambda i: settle(i, 0),
+        "p": lambda i: pass_on(i, 1),
+        "s": lambda i: settle(i, 1),
+        "X": lambda i: (start_sync, turn_sync, end_sync)[i](),
+    }
+    for step in PLAN:
+        act[step[0]](int(step[1]))
     step_rows(1)
     for copy in sent:
         copy.wait_send()

time: 131 us -> 119 us (0.908)
  Pallas kernels: 129 us -> 118 us
    pallas_call x1, Pallas kernels: 127 us -> 115 us  [on_device(): pl.pallas_call(kernel, out_shape=shapes[:2] + (jax.ShapeDtypeStruct((pad,...]
where the time goes in v5:
time: 119 us
  Pallas kernels  118 us (99%)
  between operations  1.29 us (1%)
    pallas_call x1, Pallas kernels, on_device(): pl.pallas_call(kernel, out_shape=shapes[:2] + (jax.ShapeDtypeStruct((pad,...  115 us

profile of v5, /device:TPU:1, one launch (start us, length us, event | category | flops | bytes accessed | tf_op | source)
XLA Modules:
  0.0 118.9 jit_solution(13173036156970455812)
XLA Ops:
  1.3 115.4 %shard_map.103 = (f32[1,1024]{1,0:T(1,128)}, f32[160,1024]{1,0:T(8,128)}, f32[24,1024]{1,0:T(8,128)}, f32[24,256]{1,0:T(8,128)}) custom-call(bf16[1,1024,5120]{2,1,0:T(8,128)(2,1)} %tokens.1, s32[1,1024]{1,0:T(1,128)} %targets.1, f32[1,5120]{1,0:T(1,128)} %bitcast.4, f32[160,1024]{1,0:T(8,128)} %bitcast.3, f32[160,256]{1,0:T(8,128)} %anchor.1, ...), custom_call_target="tpu_custom_call" | custom-call | tf_op jit(solution)/shard_map/pallas_call | solution.py:497
  116.7 2.2 %shard_map.104 = (f32[1,1024]{1,0:T(1,128)}, f32[160,1024]{1,0:T(8,128)}, f32[160,256]{1,0:T(8,128)}) custom-call(f32[1,1024]{1,0:T(1,128)} %get-tuple-element.10.loss, f32[160,1024]{1,0:T(8,128)} %get-tuple-element.11.stepped, f32[24,1024]{1,0:T(8,128)} %get-tuple-element.12.fresh, f32[24,256]{1,0:T(8,128)} %get-tuple-element.13.moment, ...), custom_call_target="tpu_custom_call" | custom-call | tf_op jit(solution)/shard_map/pallas_call | solution.py:531

commit v6 on v5

--- a/solution.py
+++ b/solution.py
@@ -31,10 +31,10 @@
 
 
 def kernel(
-    tokens, targets, gain, weights, anchor, momentum, step_index, frag_table,
+    tokens, targets_in, gain_in, weights_in, anchor_in, momentum_in, step_in, table_in,
     loss_out, stepped_out, fresh_out, moment_out,
     head, normed_t, grad, logits_t, err_t, tok, rq_half, rq, rx, rx_far, rp_half, rp, rolled, rows_out, rows_in, new_out, new_in,
-    tok_sem, gp_s, gp_r, gx_s, gx_r, gf_s, gf_r, gq_s, gq_r,
+    targets, gain, weights, anchor, momentum, step_index, frag_table, load_sem, tok_sem, gp_s, gp_r, gx_s, gx_r, gf_s, gf_r, gq_s, gq_r,
     sp_s, sp_r, sx_s, sx_r, sf_s, sf_r, sq_s, sq_r, e_s, e_r, n_s, n_r,
 ):
     rows, vocab = weights.shape
@@ -76,8 +76,19 @@
             tokens.at[0, pl.ds(c * chunk, chunk)], tok.at[c % slots], tok_sem.at[c % slots]
         )
 
+    pairs = (
+        (step_in, step_index), (table_in, frag_table), (weights_in, weights), (gain_in, gain),
+        (targets_in, targets), (anchor_in, anchor), (momentum_in, momentum),
+    )
+    loads = [pltpu.make_async_copy(src, dst, load_sem.at[k]) for k, (src, dst) in enumerate(pairs)]
+    for load in loads[:3]:
+        load.start()
     for c in range(slots):
         token_copy(c).start()
+    for load in loads[3:]:
+        load.start()
+    for load in loads[:3]:
+        load.wait()
     pos = step_index[0] % frag_count
     frag = jnp.int32(0)
     for k in range(frag_count):
@@ -192,6 +203,8 @@
     up = send(own, head.at[6, whole(0)], gp_s.at[0], gp_r.at[0], p_up)
     down = send(own, head.at[2, whole(0)], gp_s.at[1], gp_r.at[1], p_down)
     gx, gq, fq, gf = {0: gather_x(0)}, {0: gather_q(0)}, {}, {}
+    for load in loads[3:]:
+        load.wait()
     norm(0, 4)
     up.wait_recv()
     up2 = send(head.at[6, low(0)], head.at[4, low(0)], gp_s.at[2], gp_r.at[2], p_up)
@@ -497,7 +510,7 @@
     loss, stepped, fresh, moment = pl.pallas_call(
         kernel,
         out_shape=shapes[:2] + (jax.ShapeDtypeStruct((pad, vocab), F32), jax.ShapeDtypeStruct((pad, part), F32)),
-        in_specs=[pl.BlockSpec(memory_space=pl.ANY)] + [vmem] * 5 + [smem] * 2,
+        in_specs=[pl.BlockSpec(memory_space=pl.ANY)] * 8,
         out_specs=(vmem,) * 4,
         scratch_shapes=[
             big,
@@ -517,6 +530,14 @@
             pltpu.VMEM((3, pad, part), F32),
             pltpu.VMEM((pad, part), F32),
             pltpu.VMEM((3, pad, part), F32),
+            pltpu.VMEM((1, count), jnp.int32),
+            pltpu.VMEM((1, width), F32),
+            pltpu.VMEM((rows, vocab), F32),
+            pltpu.VMEM((rows, part), F32),
+            pltpu.VMEM((rows, part), F32),
+            pltpu.SMEM(step_index.shape, jnp.int32),
+            pltpu.SMEM(frag_table.shape, jnp.int32),
+            dma((7,)),
             dma((2,)),
             dma((4,)), dma((4,)), dma((4,)), dma((4,)), dma((4,)), dma((4,)), dma((8, 4)), dma((8, 4)),
             dma((2, 4)), dma((2, 4)), dma((2, 4)), dma((2, 4)), dma((2, 4)), dma((2, 4)), dma((2, 8, 4)), dma((2, 8, 4)),

time: 119 us -> 118 us (level)
  Pallas kernels: 118 us -> 116 us
where the time goes in v6:
time: 118 us
  Pallas kernels  116 us (98%)
  between operations  1.29 us (1%)
    pallas_call x1, Pallas kernels, on_device(): pl.pallas_call(kernel, out_shape=shapes[:2] + (jax.ShapeDtypeStruct((pad,...  114 us

profile of v6, /device:TPU:1, one launch (start us, length us, event | category | flops | bytes accessed | tf_op | source)
XLA Modules:
  0.0 117.7 jit_solution(985916143704889421)
XLA Ops:
  1.3 114.2 %shard_map.103 = (f32[1,1024]{1,0:T(1,128)}, f32[160,1024]{1,0:T(8,128)}, f32[24,1024]{1,0:T(8,128)}, f32[24,256]{1,0:T(8,128)}) custom-call(bf16[1,1024,5120]{2,1,0:T(8,128)(2,1)} %tokens.1, s32[1,1024]{1,0:T(1,128)} %targets_in.1, f32[1,5120]{1,0:T(1,128)} %bitcast.4, f32[160,1024]{1,0:T(8,128)} %bitcast.3, f32[160,256]{1,0:T(8,128)} %anchor_in.1, ...), custom_call_target="tpu_custom_call" | custom-call | tf_op jit(solution)/shard_map/pallas_call | solution.py:510
  115.5 2.2 %shard_map.104 = (f32[1,1024]{1,0:T(1,128)}, f32[160,1024]{1,0:T(8,128)}, f32[160,256]{1,0:T(8,128)}) custom-call(f32[1,1024]{1,0:T(1,128)} %get-tuple-element.10.loss, f32[160,1024]{1,0:T(8,128)} %get-tuple-element.11.stepped, f32[24,1024]{1,0:T(8,128)} %get-tuple-element.12.fresh, f32[24,256]{1,0:T(8,128)} %get-tuple-element.13.moment, ...), custom_call_target="tpu_custom_call" | custom-call | tf_op jit(solution)/shard_map/pallas_call | solution.py:552

commit v7 on v6

--- a/solution.py
+++ b/solution.py
@@ -256,14 +256,11 @@
     tail = (3, 7, 5)
     for i in tail:
         settle_q(i)
-    logits_t[...] += dot(
-        jnp.concatenate([head[i, last] for i in tail]), jnp.concatenate([normed_t[i, last] for i in tail]), 0, 0
-    )
 
     lanes = 128
 
     def soften(j, carry):
-        s = pl.ds(pl.multiple_of(j * lanes, lanes), lanes)
+        s = pl.ds(j * lanes, lanes)
         logit = logits_t[:, s] * scale
         expo = jnp.exp(logit)
         total = jnp.sum(expo, axis=0, keepdims=True)
@@ -273,7 +270,14 @@
         err_t[:, s] = (expo * (1.0 / total) - jnp.where(onehot, 1.0, 0.0)).astype(BF16)
         return carry
 
-    lax.fori_loop(0, count // lanes, soften, 0)
+    late_head = jnp.concatenate([head[i, last] for i in tail])
+    parts = 2
+    for k in range(parts):
+        s = pl.ds(k * count // parts, count // parts)
+        late_tokens = jnp.concatenate([normed_t[i, last, s] for i in tail])
+        logits_t[:, s] += dot(late_head, late_tokens, 0, 0)
+        for j in range(count // parts // lanes):
+            soften(k * (count // parts // lanes) + j, 0)
 
     def terms(i, slot):
         two = pl.ds(slot * rows, 2 * rows)

time: 118 us -> 117 us (level)
  no operation moved by 1% of the time
where the time goes in v7:
time: 117 us
  Pallas kernels  115 us (98%)
  between operations  1.29 us (1%)
    pallas_call x1, Pallas kernels, on_device(): pl.pallas_call(kernel, out_shape=shapes[:2] + (jax.ShapeDtypeStruct((pad,...  113 us

profile of v7, /device:TPU:1, one launch (start us, length us, event | category | flops | bytes accessed | tf_op | source)
XLA Modules:
  0.0 116.6 jit_solution(11954877505525349892)
XLA Ops:
  1.3 113.1 %shard_map.103 = (f32[1,1024]{1,0:T(1,128)}, f32[160,1024]{1,0:T(8,128)}, f32[24,1024]{1,0:T(8,128)}, f32[24,256]{1,0:T(8,128)}) custom-call(bf16[1,1024,5120]{2,1,0:T(8,128)(2,1)} %tokens.1, s32[1,1024]{1,0:T(1,128)} %targets_in.1, f32[1,5120]{1,0:T(1,128)} %bitcast.4, f32[160,1024]{1,0:T(8,128)} %bitcast.3, f32[160,256]{1,0:T(8,128)} %anchor_in.1, ...), custom_call_target="tpu_custom_call" | custom-call | tf_op jit(solution)/shard_map/pallas_call | solution.py:514
  114.4 2.2 %shard_map.104 = (f32[1,1024]{1,0:T(1,128)}, f32[160,1024]{1,0:T(8,128)}, f32[160,256]{1,0:T(8,128)}) custom-call(f32[1,1024]{1,0:T(1,128)} %get-tuple-element.10.loss, f32[160,1024]{1,0:T(8,128)} %get-tuple-element.11.stepped, f32[24,1024]{1,0:T(8,128)} %get-tuple-element.12.fresh, f32[24,256]{1,0:T(8,128)} %get-tuple-element.13.moment, ...), custom_call_target="tpu_custom_call" | custom-call | tf_op jit(solution)/shard_map/pallas_call | solution.py:556

commit v8 on v7

--- a/solution.py
+++ b/solution.py
@@ -13,7 +13,7 @@
 MESH = pl.DeviceIdType.MESH
 
 PLAN = (
-    "T7", "h7", "T3", "P7", "h3", "T5", "h5", "p7",
+    "Z7", "T3", "P7", "h3", "T5", "h5", "p7",
     "T1", "p5", "h1", "T2", "h2", "T4", "p3", "T6",
     "P1", "T0", "P3", "S7", "P4", "h6", "P6", "S1",
     "h0", "P0", "S4", "s5", "P2", "p1", "h4", "S6",
@@ -261,11 +261,11 @@
 
     def soften(j, carry):
         s = pl.ds(j * lanes, lanes)
-        logit = logits_t[:, s] * scale
-        expo = jnp.exp(logit)
+        raw = logits_t[:, s]
+        expo = jnp.exp2(raw * np.float32(scale / np.log(2.0)))
         total = jnp.sum(expo, axis=0, keepdims=True)
         onehot = lax.broadcasted_iota(jnp.int32, (vocab, lanes), 0) == targets[:, s]
-        picked = jnp.sum(jnp.where(onehot, logit, 0.0), axis=0, keepdims=True)
+        picked = jnp.sum(jnp.where(onehot, raw, 0.0), axis=0, keepdims=True) * scale
         loss_out[:, s] = jnp.log(total) - picked
         err_t[:, s] = (expo * (1.0 / total) - jnp.where(onehot, 1.0, 0.0)).astype(BF16)
         return carry
@@ -343,6 +343,15 @@
         start_halves(i, 0)
         terms(i, 0)
         give_far(i, 0, 1, 0)
+
+    def start_both(i):
+        terms(i, 2)
+        for part in range(2):
+            give_far(i, part, 2, 3)
+            start_halves(i, part)
+        terms(i, 0)
+        for part in range(2):
+            give_far(i, part, 1, 0)
 
     def start_rest(i):
         give_far(i, 1, 2)
@@ -454,6 +463,7 @@
     act = {
         "T": start_terms,
         "h": start_rest,
+        "Z": start_both,
         "P": lambda i: pass_on(i, 0),
         "S": lambda i: settle(i, 0),
         "p": lambda i: pass_on(i, 1),

time: 117 us -> 116 us (level)
  no operation moved by 1% of the time
where the time goes in v8:
time: 116 us
  Pallas kernels  115 us (99%)
  between operations  1.29 us (1%)
    pallas_call x1, Pallas kernels, on_device(): pl.pallas_call(kernel, out_shape=shapes[:2] + (jax.ShapeDtypeStruct((pad,...  113 us

profile of v8, /device:TPU:1, one launch (start us, length us, event | category | flops | bytes accessed | tf_op | source)
XLA Modules:
  0.0 116.2 jit_solution(7228670384129507240)
XLA Ops:
  1.3 112.8 %shard_map.103 = (f32[1,1024]{1,0:T(1,128)}, f32[160,1024]{1,0:T(8,128)}, f32[24,1024]{1,0:T(8,128)}, f32[24,256]{1,0:T(8,128)}) custom-call(bf16[1,1024,5120]{2,1,0:T(8,128)(2,1)} %tokens.1, s32[1,1024]{1,0:T(1,128)} %targets_in.1, f32[1,5120]{1,0:T(1,128)} %bitcast.4, f32[160,1024]{1,0:T(8,128)} %bitcast.3, f32[160,256]{1,0:T(8,128)} %anchor_in.1, ...), custom_call_target="tpu_custom_call" | custom-call | tf_op jit(solution)/shard_map/pallas_call | solution.py:524
  114.1 2.2 %shard_map.104 = (f32[1,1024]{1,0:T(1,128)}, f32[160,1024]{1,0:T(8,128)}, f32[160,256]{1,0:T(8,128)}) custom-call(f32[1,1024]{1,0:T(1,128)} %get-tuple-element.10.loss, f32[160,1024]{1,0:T(8,128)} %get-tuple-element.11.stepped, f32[24,1024]{1,0:T(8,128)} %get-tuple-element.12.fresh, f32[24,256]{1,0:T(8,128)} %get-tuple-element.13.moment, ...), custom_call_target="tpu_custom_call" | custom-call | tf_op jit(solution)/shard_map/pallas_call | solution.py:566
